TPU v7x, 128 devices: a whole 4x4x4 slice. The times are simulated.
128 devices in a mesh: fsdp: 16 (over x, y_hi, core), user: 8 (over y_lo, z).
Axes of the slice: x: 4, y: 4 (y_hi: 2, y_lo: 2; y = y_hi * 2 + y_lo), z: 4, core: 2. Of those that a mesh axis runs over, the one named last changes fastest.
Arguments:
- gate_pre: bfloat16 [16384, 18432], P('fsdp', 'user'), may hold values from -6 to 6
- up_pre: bfloat16 [16384, 18432], P('fsdp', 'user'), may hold values from -6 to 6
- out_grad: bfloat16 [16384, 2304], P(('fsdp', 'user')), may hold values from -16 to 16
- down_weight: bfloat16 [18432, 2304], P('user', 'fsdp'), may hold values from -0.046875 to 0.046875
- token_user: int32 [16384, 1], P('fsdp'), may hold values from 0 to 15, as said below
- noise: float32 [18432, 2304], P('user', 'fsdp'), may hold values from -1.5 to 1.5
Outputs:
- gate_grad: bfloat16 [16384, 18432], P('fsdp', 'user')
- up_grad: bfloat16 [16384, 18432], P('fsdp', 'user')
- weight_update: float32 [18432, 2304], P('user', 'fsdp')
Inputs may be any that keep to these rules, and one draw needn't show every extreme that they name: `token_user`: within the rows of one group (1024 rows, one index of fsdp) no user is named by more than 128 rows, and some user by exactly 128.
All inputs are finite; a program needn't handle non-finite values.
Results may differ from a plain program's by a relative error of at most 0.01.
Values may be sent and summed in bfloat16 or wider, within the bound.
No kernel may reach another device: no remote copies, remote signals or barrier semaphores. Data moves between devices by JAX's collectives and lax.ppermute only.
A program may use at most 256 MiB of HBM per device.

v0:
```python
import math

import jax
import jax.numpy as jnp
from jax import lax
from jax.sharding import PartitionSpec as P

D = 2304
F = 18432
SLOTS = 128
USR_DEV = 2


root_two_pi = math.sqrt(2.0 / math.pi)


def gelu_parts(gate):
    inner_term = gate + 0.044715 * gate * gate * gate
    tanh_value = jnp.tanh(root_two_pi * inner_term)
    gelu_value = 0.5 * gate * (1.0 + tanh_value)
    gelu_slope = 0.5 * (1.0 + tanh_value) + 0.5 * gate * (
        1.0 - tanh_value * tanh_value
    ) * root_two_pi * (1.0 + 3.0 * 0.044715 * gate * gate)
    return (gelu_value, gelu_slope)


def slot_layout(user_of_row, users_group):
    row_count = user_of_row.shape[0]
    onehot = (user_of_row[:, None] == jnp.arange(users_group, dtype=jnp.int32)[None, :]).astype(
        jnp.int32
    )
    row_rank = jnp.sum((jnp.cumsum(onehot, axis=0) - onehot) * onehot, axis=1)
    target = user_of_row * SLOTS + row_rank
    slot_rows = (
        jnp.zeros((users_group * SLOTS,), jnp.int32)
        .at[target]
        .set(jnp.arange(row_count, dtype=jnp.int32))
    )
    filled = jnp.zeros((users_group * SLOTS,), jnp.float32).at[target].set(1.0)
    return (
        slot_rows.reshape(users_group, SLOTS),
        filled.reshape(users_group, SLOTS),
        onehot.astype(jnp.float32),
    )


def slot_gram(values, slot_rows, slot_mask):
    gathered = jnp.take(values, slot_rows, axis=0) * slot_mask
    return jnp.einsum("usf,utf->ust", gathered, gathered, preferred_element_type=jnp.float32)


def local(gate_pre, up_pre, out_grad, down_weight, token_user, noise):
    n_user = lax.axis_size("user")
    n_fsdp = lax.axis_size("fsdp")
    users_group = USR_DEV * n_user
    clip_bound = 0.5 * math.sqrt(SLOTS * F * D)
    user_of_row = token_user[:, 0]
    gate_f = gate_pre.astype(jnp.float32)
    up_f = up_pre.astype(jnp.float32)
    gelu_value, gelu_slope = gelu_parts(gate_f)
    hidden = (gelu_value * up_f).astype(jnp.bfloat16)
    grad_rows = lax.all_gather(out_grad, "user", axis=0, tiled=True)
    columns = grad_rows
    hidden_grad = lax.dot_general(
        columns,
        lax.all_gather(down_weight, "fsdp", axis=1, tiled=True),
        (((1,), (1,)), ((), ())),
        preferred_element_type=jnp.float32,
    )
    gate_grad = (hidden_grad * up_f * gelu_slope).astype(jnp.bfloat16)
    up_grad = (hidden_grad * gelu_value).astype(jnp.bfloat16)
    slot_rows, filled, onehot = slot_layout(user_of_row, users_group)
    slot_mask = filled.astype(jnp.bfloat16)[:, :, None]
    hidden_gram = slot_gram(hidden, slot_rows, slot_mask)
    grad_gram = slot_gram(grad_rows, slot_rows, slot_mask)
    partial_squares = jnp.sum(hidden_gram * grad_gram, axis=(1, 2))
    squares = lax.psum(partial_squares, "user")
    factor = clip_bound / jnp.maximum(jnp.sqrt(squares), clip_bound)
    row_factor = jnp.sum(onehot * factor[None, :], axis=1)
    scaled = (grad_rows.astype(jnp.float32) * row_factor[:, None]).astype(jnp.bfloat16)
    scale = math.sqrt(F * D) / (users_group * n_fsdp * clip_bound)
    columns = scaled
    summed = (
        lax.psum_scatter(
            lax.dot_general(
                columns, hidden, (((0,), (0,)), ((), ())), preferred_element_type=jnp.float32
            ).astype(jnp.bfloat16),
            "fsdp",
            scatter_dimension=0,
            tiled=True,
        )
        .astype(jnp.float32)
        .T
    )
    weight_update = scale * summed + noise
    return (gate_grad, up_grad, weight_update)


def solution(mesh):
    return jax.shard_map(
        local,
        mesh=mesh,
        in_specs=(
            P("fsdp", "user"),
            P("fsdp", "user"),
            P(("fsdp", "user"), None),
            P("user", "fsdp"),
            P("fsdp", None),
            P("user", "fsdp"),
        ),
        out_specs=(P("fsdp", "user"), P("fsdp", "user"), P("user", "fsdp")),
        check_vma=False,
    )
```

profile of v0, /device:TPU:0, one launch (start us, length us, event | category | flops | bytes accessed | tf_op | source)
XLA Modules:
  0.0 365.7 jit_solution(4948925078979433067)
XLA Ops:
  7.2 0.7 all-gather.3.cloned.1.call-update
  7.9 0.7 all-gather.5.cloned.1.call-update
  8.7 0.7 fusion.26
  9.4 4.5 %reduce-window.6 = s32[16,8,128]{2,1,0:T(8,128)S(1)} reduce-window(s32[16,8,128]{2,1,0:T(8,128)S(1)} %fusion.26, s32[]{:T(128)} %constant.6.clone.1), window={size=1x1x128 pad=0_0x0_0x127_0}, to_apply=%region_0.0 | reduce-window | flops 2080768 | bytes 131076 | tf_op jit(solution)/shard_map/reduce-window
  13.9 0.1 slice.12
  14.0 0.1 copy.11
  14.1 0.1 copy.12
  14.2 0.1 broadcast_add_fusion
  14.3 0.7 fusion.23
  15.0 0.7 compare_select_fusion
  15.7 4.3 %scatter_custom_fusion = s32[2048]{0:T(1024)S(1)} fusion(s32[1024]{0:T(1024)S(1)} %bitcast.40, s32[1024]{0:T(1024)S(1)} %iota.11, s32[]{:T(128)} %constant.6.clone.1), kind=kCustom, calls=%fused_computation.59 | custom fusion | bytes 8196 | tf_op jit(solution)/shard_map/scatter | solution.py:37
  20.1 4.3 %scatter_custom_fusion.1 = f32[2048]{0:T(1024)S(1)} fusion(s32[1024]{0:T(1024)S(1)} %bitcast.41, f32[1024]{0:T(1024)S(1)} %broadcast.50, f32[]{:T(128)} %constant.9.clone.1), kind=kCustom, calls=%fused_computation.57 | custom fusion | bytes 8196 | tf_op jit(solution)/shard_map/scatter | solution.py:39
  24.4 45.4 %all-gather.3.cloned.1.call-done = bf16[1024,2304]{1,0:T(8,128)(2,1)} async-done(((bf16[128,2304]{1,0:T(8,128)(2,1)}), bf16[1024,2304]{1,0:T(8,128)(2,1)}) %all-gather.3.cloned.1.call-update) | async-done | bytes 4718608 | tf_op jit(solution)/shard_map/all_gather | solution.py:62
  69.9 21.4 %gather_fusion.1 = bf16[2048,2304]{1,0:T(8,128)(2,1)} fusion(bf16[1024,2304]{1,0:T(8,128)(2,1)} %all-gather.3.cloned.1.call-done, s32[2048]{0:T(1024)S(1)} %bitcast_clamp_fusion), kind=kCustom, calls=%fused_computation.1.clone | custom fusion | bytes 18882560 | tf_op jit(solution)/shard_map/jit(_take)/gather | solution.py:48
  91.2 10.0 %fusion.11 = f32[16,128,128]{2,1,0:T(8,128)S(1)} fusion(bf16[16,128,2304]{2,1,0:T(8,128)(2,1)} %bitcast.33, pred[16,128]{1,0:T(8,128)(4,1)S(1)} %compare_and_fusion, bf16[16,128]{1,0:T(8,128)(2,1)S(1)} %convert_bitcast_fusion), kind=kOutput, calls=%fused_computation.26 | convolution fusion | flops 1217396736 | bytes 10491904 | tf_op jit(solution)/shard_map/usf,utf->ust/dot_general | solution.py:49
  101.2 51.7 %all-gather.5.cloned.1.call-done = bf16[2304,2304]{0,1:T(8,128)(2,1)} async-done(((bf16[2304,144]{0,1:T(8,128)(2,1)}), bf16[2304,2304]{0,1:T(8,128)(2,1)}) %all-gather.5.cloned.1.call-update) | async-done | bytes 10616848 | tf_op jit(solution)/shard_map/all_gather | solution.py:66
  152.9 27.7 %multiply_convert_fusion.1 = (bf16[1024,2304]{1,0:T(8,128)(2,1)}, bf16[1024,2304]{1,0:T(8,128)(2,1)}, bf16[1024,2304]{1,0:T(8,128)(2,1)}) fusion(bf16[1024,2304]{1,0:T(8,128)(2,1)} %param.8, bf16[1024,2304]{1,0:T(8,128)(2,1)} %param.9, bf16[1024,2304]{1,0:T(8,128)(2,1)} %all-gather.3.cloned.1.call-done, bf16[2304,2304]{0,1:T(8,128)(2,1)} %all-gather.5.cloned.1.call-done), kind=kOutput, calls=%fused_computation.30 | convolution fusion | flops 10935336960 | bytes 38928384 | tf_op jit(solution)/shard_map/dot_general | solution.py:64
  180.6 21.2 %gather_fusion = bf16[2048,2304]{1,0:T(8,128)(2,1)} fusion(bf16[1024,2304]{1,0:T(8,128)(2,1)} %get-tuple-element.6, s32[2048]{0:T(1024)S(1)} %bitcast_clamp_fusion), kind=kCustom, calls=%fused_computation.clone | custom fusion | bytes 18882560 | tf_op jit(solution)/shard_map/jit(_take)/gather | solution.py:48
  201.9 9.9 %fusion.21 = f32[16]{0:T(128)S(1)} fusion(f32[16,128,128]{2,1,0:T(8,128)S(1)} %fusion.11, bf16[16,128,2304]{2,1,0:T(8,128)(2,1)} %bitcast.32, pred[16,128]{1,0:T(8,128)(4,1)S(1)} %compare_and_fusion, bf16[16,128]{1,0:T(8,128)(2,1)S(1)} %convert_bitcast_fusion), kind=kOutput, calls=%fused_computation.40 | convolution fusion | flops 1217921024 | bytes 10491968 | tf_op jit(solution)/shard_map/usf,utf->ust/dot_general | solution.py:49
  211.8 18.9 %psum.7 = f32[16]{0:T(128)S(1)} all-reduce(f32[16]{0:T(128)S(1)} %fusion.21), channel_id=1, replica_groups=mesh['fsdp'=16,'user'=8] {'user'}, use_global_device_ids=true, to_apply=%region_6.8 | all-reduce | flops 16 | bytes 128 | tf_op jit(solution)/shard_map/psum | solution.py:77
  230.7 0.1 fusion.25
  230.8 17.1 %convolution_convert_fusion = bf16[2304,2304]{1,0:T(8,128)(2,1)} fusion(bf16[1024,2304]{1,0:T(8,128)(2,1)} %get-tuple-element.6, bf16[1024,2304]{1,0:T(8,128)(2,1)} %all-gather.3.cloned.1.call-done, f32[1024]{0:T(1024)S(1)} %fusion.25), kind=kOutput, calls=%fused_computation.11 | convolution fusion | flops 10884022272 | bytes 20058112 | tf_op jit(solution)/shard_map/dot_general | solution.py:85
  248.0 109.0 %reduce-scatter.2.cloned.1.call-done = bf16[144,2304]{1,0:T(8,128)(2,1)} async-done(((bf16[2304,2304]{1,0:T(8,128)(2,1)}), bf16[144,2304]{1,0:T(8,128)(2,1)}) %reduce-scatter.2.cloned.1.call-update) | async-done | bytes 663568 | tf_op jit(solution)/shard_map/reduce_scatter | solution.py:84
  356.9 2.3 bitcast_add_fusion
  (16 shorter events, 0.2 us)
Async XLA Ops:
  7.2 62.7 %all-gather.3.cloned.1.call-start = ((), (), s32[]{:S(2)}) async-start(), calls=%async_computation.1 | async-start | bytes 5308416 | tf_op jit(solution)/shard_map/all_gather | solution.py:62
  7.9 145.0 %all-gather.5.cloned.1.call-start = ((), (), s32[]{:S(2)}) async-start(), calls=%async_computation.2 | async-start | bytes 11280384 | tf_op jit(solution)/shard_map/all_gather | solution.py:66
  8.6 348.3 %reduce-scatter.2.cloned.1.call-start = ((), (), s32[]{:S(2)}) async-start(), calls=%async_computation.3 | async-start | bytes 11280384 | tf_op jit(solution)/shard_map/reduce_scatter | solution.py:84
  201.9 28.9 %copy-start.1 = (s32[1024,1]{0,1:T(1,128)S(1)}, s32[1024,1]{0,1:T(1,128)}, u32[]{:S(2)}) copy-start(s32[1024,1]{0,1:T(1,128)} %param.12) | copy-start | bytes 12292
  247.9 109.0 %copy-start = (f32[2304,144]{0,1:T(8,128)S(1)}, f32[2304,144]{0,1:T(8,128)}, u32[]{:S(2)}) copy-start(f32[2304,144]{0,1:T(8,128)} %param.13) | copy-start | bytes 3981316
Sparse Core Ops, SparseCore 0:
  9.6 60.1 all-gather.2
  72.3 80.6 all-gather.4
  248.1 108.7 reduce-scatter.1
where the time goes:
time: 366 us
  waiting for transfers between devices  208 us (57%)
  matrix products  64.7 us (18%)
  local copies, waits for them, and re-layouts  51.5 us (14%)
  blocking collectives  18.9 us (5%)
  between operations  13.8 us (4%)
  other arithmetic  9.12 us (2%)
    reduce_scatter x1, waiting for transfers between devices, local(): lax.psum_scatter(lax.dot_general(columns, hidden, (((0,), (0,)), ((), ())...  109 us
    all_gather x1, waiting for transfers between devices, local(): lax.all_gather(down_weight, 'fsdp', axis=1, tiled=True)  51.7 us
    all_gather x1, waiting for transfers between devices, local(): grad_rows = lax.all_gather(out_grad, 'user', axis=0, tiled=True)  45.4 us
    gather x2, local copies, waits for them, and re-layouts, slot_gram(): gathered = jnp.take(values, slot_rows, axis=0) * slot_mask  42.6 us
    dot_general x1, matrix products, local(): lax.dot_general(columns, lax.all_gather(down_weight, 'fsdp', axis=1, tile...  27.7 us
    dot_general x2, matrix products, slot_gram(): jnp.einsum('usf,utf->ust', gathered, gathered, preferred_element_type=jnp...  19.9 us
    psum x1, blocking collectives, local(): squares = lax.psum(partial_squares, 'user')  18.9 us
    dot_general x1, matrix products, local(): lax.dot_general(columns, hidden, (((0,), (0,)), ((), ())), preferred_elem...  17.1 us
  transfers between devices with their start and end apart: 3, of which 3 were waited for; matrix products, arithmetic and copies ran while one was open for 13% of the time, Pallas kernels for 0%

commit v1 on v0

v1 whole, which is shorter than its diff:
```python
import functools
import math

import jax
import jax.numpy as jnp
from jax import lax
from jax.experimental import pallas as pl
from jax.experimental.pallas import tpu as pltpu
from jax.sharding import Mesh, PartitionSpec as P

D = 2304
F = 18432
SLOTS = 128
USR_DEV = 2
NX, NY, NC, NP, NZ = 4, 2, 2, 2, 4
TILE = 256
MIB = 2**20

root_two_pi = math.sqrt(2.0 / math.pi)
VMEM = pl.BlockSpec(memory_space=pltpu.VMEM)
SMEM = pl.BlockSpec(memory_space=pltpu.SMEM)
ANY = pl.BlockSpec(memory_space=pl.ANY)


def gelu_parts(gate):
    square = gate * gate
    tanh_value = jnp.tanh(gate * (root_two_pi + (root_two_pi * 0.044715) * square))
    share = 0.5 + 0.5 * tanh_value
    gelu_slope = share + (0.5 * gate) * (1.0 - tanh_value * tanh_value) * (
        root_two_pi + (root_two_pi * 3.0 * 0.044715) * square
    )
    return (gate * share, gelu_slope)


def shift(count, by):
    return [(i, (i + by) % count) for i in range(count)]


LITTLE = pl.CostEstimate(flops=1, bytes_accessed=1, transcendentals=0)
TOKEN = jax.ShapeDtypeStruct((8, 128), jnp.float32)


def params(mib, *semantics):
    return pltpu.CompilerParams(
        vmem_limit_bytes=mib * MIB, dimension_semantics=semantics or None
    )


def hidden_kernel(gate_ref, up_ref, hidden_ref):
    gelu_value, _ = gelu_parts(gate_ref[...].astype(jnp.float32))
    hidden_ref[...] = (gelu_value * up_ref[...].astype(jnp.float32)).astype(jnp.bfloat16)


def hidden_call(gate, up):
    rows, cols = gate.shape
    spec = pl.BlockSpec((TILE // 2, cols), lambda i: (i, 0))
    return pl.pallas_call(
        hidden_kernel,
        grid=(2 * rows // TILE,),
        in_specs=[spec, spec],
        out_specs=spec,
        out_shape=jax.ShapeDtypeStruct(gate.shape, jnp.bfloat16),
        compiler_params=params(40, "arbitrary"),
        cost_estimate=LITTLE,
        name="hidden",
    )(gate, up)


def tiles_of(rows):
    count = rows // TILE
    return [(i, j) for i in range(count) for j in range(i, count)]


def outer(left, right):
    return lax.dot_general(
        left, right, (((1,), (1,)), ((), ())), preferred_element_type=jnp.float32
    )


def hidden_gram_kernel(hidden_ref, user_ref, user_row_ref, gram_ref):
    for k, (i, j) in enumerate(tiles_of(hidden_ref.shape[0])):
        first, second = pl.ds(i * TILE, TILE), pl.ds(j * TILE, TILE)
        tile = outer(hidden_ref[first, :], hidden_ref[second, :])
        same = user_ref[first, :] == user_row_ref[:, second]
        gram_ref[k] = jnp.where(same, tile if i == j else 2.0 * tile, 0.0)


def hidden_gram_call(hidden, user, user_row):
    rows, cols = hidden.shape
    count = len(tiles_of(rows))
    return pl.pallas_call(
        hidden_gram_kernel,
        in_specs=[VMEM, VMEM, VMEM],
        out_specs=VMEM,
        out_shape=jax.ShapeDtypeStruct((count, TILE, TILE), jnp.float32),
        compiler_params=params(24),
        cost_estimate=LITTLE,
        name="hidden_gram",
    )(hidden, user, user_row)


def grad_gram_kernel(place_ref, *refs):
    count = len(refs) - 5
    pieces = refs[:count]
    gram_ref, user_row_ref, grad_ref, squares_ref, sems = refs[count:]
    copies = []
    for k, piece in enumerate(pieces):
        size = piece.shape[0]
        start = pl.multiple_of(place_ref[k + 3], size)
        copies.append(pltpu.make_async_copy(piece, grad_ref.at[pl.ds(start, size)], sems.at[k]))
    for copy in copies:
        copy.start()
    for copy in copies:
        copy.wait()
    rows = grad_ref.shape[0]
    terms = [None] * (rows // TILE)
    for k, (i, j) in enumerate(tiles_of(rows)):
        tile = outer(grad_ref[pl.ds(i * TILE, TILE), :], grad_ref[pl.ds(j * TILE, TILE), :])
        term = jnp.sum(tile * gram_ref[k], axis=0, keepdims=True)
        terms[j] = term if terms[j] is None else terms[j] + term
    terms = jnp.concatenate(terms, axis=1)
    users = lax.broadcasted_iota(jnp.int32, (squares_ref.shape[0], rows), 0)
    chosen = jnp.where(users == user_row_ref[...], terms, 0.0)
    squares_ref[...] = jnp.broadcast_to(
        jnp.sum(chosen, axis=1, keepdims=True), squares_ref.shape
    )


def grad_gram_call(place, pieces, gram, user_row, users_group):
    rows, cols = user_row.shape[1], pieces[0].shape[1]
    return pl.pallas_call(
        grad_gram_kernel,
        in_specs=[SMEM] + [ANY] * len(pieces) + [VMEM] * 2,
        out_specs=[VMEM] * 2,
        out_shape=[
            jax.ShapeDtypeStruct((rows, cols), jnp.bfloat16),
            jax.ShapeDtypeStruct((users_group, 128), jnp.float32),
        ],
        scratch_shapes=[pltpu.SemaphoreType.DMA((len(pieces),))],
        compiler_params=params(40),
        cost_estimate=LITTLE,
        name="grad_gram",
    )(place, *pieces, gram, user_row)


def transpose_kernel(place_ref, grad_ref, mine_ref, other_ref):
    core = place_ref[0]
    count, width, _ = mine_ref.shape
    turned = grad_ref[...].T
    for k in range(count):
        first, second = (turned[(2 * k + i) * width : (2 * k + i + 1) * width] for i in range(2))
        mine_ref[k] = jnp.where(core == 0, first, second)
        other_ref[k] = jnp.where(core == 0, second, first)


def transpose_call(place, grad, width):
    rows, cols = grad.shape
    count = cols // width // NC
    out = pl.BlockSpec((count // 2, width, rows), lambda i: (i, 0, 0))
    return pl.pallas_call(
        transpose_kernel,
        grid=(2,),
        in_specs=[SMEM, pl.BlockSpec((rows, cols // 2), lambda i: (0, i))],
        out_specs=[out, out],
        out_shape=[jax.ShapeDtypeStruct((count, width, rows), grad.dtype)] * 2,
        compiler_params=params(40, "arbitrary"),
        cost_estimate=LITTLE,
        name="transpose",
    )(place, grad)


def scale_rows(
    clip_bound, place_ref, mine_ref, theirs_ref, squares_ref, more_ref, user_refs, scaled_ref
):
    width, rows = mine_ref.shape[1:]
    count = squares_ref.shape[0] // 2
    ids = lax.broadcasted_iota(jnp.int32, (count, rows), 0)
    x_index, y_index = place_ref[1], place_ref[2]
    for group, ref in enumerate((mine_ref, theirs_ref)):
        inside = pl.ds(group * count, count)
        squares = squares_ref[inside, 0:1] + more_ref[inside, 0:1]
        factor = clip_bound / jnp.maximum(jnp.sqrt(squares), clip_bound)
        chosen = jnp.where(ids == user_refs[group][...], factor, 0.0)
        row_factor = jnp.sum(chosen, axis=0, keepdims=True)
        for dx in range(NX):
            for dy in range(NY):
                block = ref[((x_index + dx) % NX) * NY + (y_index + dy) % NY]
                scaled_ref[
                    pl.ds((dx * NY + dy) * width, width), pl.ds(group * rows, rows)
                ] = (block.astype(jnp.float32) * row_factor).astype(jnp.bfloat16)


def term_kernel(
    clip_bound, by_x, place_ref, mine_ref, theirs_ref, own_ref, sib_ref, squares_ref, more_ref,
    user_ref, user_sib_ref, after_ref, *refs
):
    outs, token_ref, scaled_ref = refs[:-2], refs[-2], refs[-1]
    token_ref[...] = jnp.zeros_like(token_ref)

    @pl.when(pl.program_id(0) == 0)
    def _():
        scale_rows(
            clip_bound, place_ref, mine_ref, theirs_ref, squares_ref, more_ref,
            (user_ref, user_sib_ref), scaled_ref,
        )

    rows = own_ref.shape[0]
    total = jnp.dot(scaled_ref[:, :rows], own_ref[...], preferred_element_type=jnp.float32)
    total += jnp.dot(scaled_ref[:, rows:], sib_ref[...], preferred_element_type=jnp.float32)
    total = total.astype(jnp.bfloat16)
    size = mine_ref.shape[1]
    for dx in range(NX):
        for dy in range(NY):
            out, at = (outs[dx], dy) if by_x else (outs[2 * dy + dx // 2], dx % 2)
            out[pl.ds(at * size, size), :] = total[(dx * NY + dy) * size :][:size]


def term_call(
    by_x, place, mine, theirs, own, sib, squares, more, user_row, user_sib, clip_bound, start, cols,
    after
):
    count, width, rows = mine.shape
    whole = lambda a: pl.BlockSpec(a.shape, lambda n: (0,) * a.ndim)
    hidden = pl.BlockSpec((rows, TILE), lambda n: (0, n + start // TILE))
    pieces = NX if by_x else 2 * NY
    size = count * width // pieces
    small = [squares, more, user_row, user_sib]
    return pl.pallas_call(
        functools.partial(term_kernel, clip_bound, by_x),
        grid=(cols // TILE,),
        in_specs=[SMEM, whole(mine), whole(theirs), hidden, hidden] + [whole(a) for a in small] + [ANY],
        out_specs=[pl.BlockSpec((size, TILE), lambda n: (0, n))] * pieces + [whole(TOKEN)],
        out_shape=[jax.ShapeDtypeStruct((size, cols), jnp.bfloat16)] * pieces + [TOKEN],
        scratch_shapes=[pltpu.VMEM((count * width, 2 * rows), jnp.bfloat16)],
        compiler_params=params(40, "arbitrary"),
        cost_estimate=LITTLE,
        name="term_x" if by_x else "term_y",
    )(place, mine, theirs, own, sib, *small, after)


def add_x_kernel(*refs):
    parts, (_, keep_ref, send_ref) = refs[:-3], refs[-3:]
    width = keep_ref.shape[0]
    total = parts[0][...].astype(jnp.float32)
    for part in parts[1:]:
        total += part[...].astype(jnp.float32)
    keep_ref[...] = total[:width]
    send_ref[...] = total[width:].astype(jnp.bfloat16)


def add_y_kernel(first_low, first_high, second_low, second_high, after_ref, *outs):
    width = outs[0].shape[0]
    for half, (first, second) in enumerate(((first_low, second_low), (first_high, second_high))):
        total = first[...].astype(jnp.float32) + second[...].astype(jnp.float32)
        for k in range(2):
            out = outs[2 * half + k]
            out[...] = total[k * width : (k + 1) * width].astype(out.dtype)


def add_call(kernel, parts, width, sends, extra=()):
    cols = parts[0].shape[1]
    tile = lambda rows: pl.BlockSpec((rows, cols // 2), lambda n: (0, n))
    return pl.pallas_call(
        kernel,
        grid=(2,),
        in_specs=[tile(a.shape[0]) for a in parts] + [ANY] * len(extra),
        out_specs=[tile(width)] * (sends + 1),
        out_shape=[jax.ShapeDtypeStruct((width, cols), jnp.float32)]
        + [jax.ShapeDtypeStruct((width, cols), jnp.bfloat16)] * sends,
        compiler_params=params(56, "arbitrary"),
        cost_estimate=LITTLE,
        name="add",
    )(*parts, *extra)


def grads_kernel(place_ref, grad_ref, same_ref, other_ref, gate_ref, up_ref, *refs):
    gate_grad_ref, up_grad_ref, token_ref, weight_ref = refs[-4:]
    width = weight_ref.shape[0] // (NX * NY * NC)
    y_index = place_ref[2]
    for k in range(NX * NC):
        x, core = k // NC, k % NC
        for ref, y in ((same_ref, y_index), (other_ref, 1 - y_index)):
            start = pl.multiple_of(((x * NY + y) * NC + core) * width, width)
            weight_ref[pl.ds(start, width), :] = ref[pl.ds(k * width, width), :]
    token_ref[...] = jnp.zeros_like(token_ref)
    hidden_grad = jnp.dot(grad_ref[...], weight_ref[...], preferred_element_type=jnp.float32)
    gelu_value, gelu_slope = gelu_parts(gate_ref[...].astype(jnp.float32))
    gate_grad_ref[...] = (hidden_grad * up_ref[...].astype(jnp.float32) * gelu_slope).astype(
        jnp.bfloat16
    )
    up_grad_ref[...] = (hidden_grad * gelu_value).astype(jnp.bfloat16)


def grads_call(place, grad, weights, gate, up, after, first, steps, held):
    rows, depth = grad.shape
    cols = gate.shape[1]
    weight = pl.BlockSpec((depth // 2, TILE), lambda n: (0, n + first))
    tile = pl.BlockSpec((rows, TILE), lambda n: (0, n + first))
    return pl.pallas_call(
        grads_kernel,
        grid=(steps,),
        in_specs=[
            SMEM,
            pl.BlockSpec((rows, depth), lambda n: (0, 0)),
            weight,
            weight,
            tile,
            tile,
            ANY,
        ]
        + [ANY] * len(held),
        out_specs=[tile, tile, pl.BlockSpec(TOKEN.shape, lambda n: (0, 0))],
        out_shape=[jax.ShapeDtypeStruct((rows, cols), jnp.bfloat16)] * 2 + [TOKEN],
        scratch_shapes=[pltpu.VMEM((depth, TILE), jnp.bfloat16)],
        input_output_aliases={7 + k: k for k in range(len(held))},
        compiler_params=params(56, "arbitrary"),
        cost_estimate=LITTLE,
        name="grads",
    )(place, grad, *weights, gate, up, after, *held)


def update_kernel(scale, own_x, got_x, own_y, *refs):
    got_y, noise_ref, out_ref = refs[:-3], refs[-3], refs[-1]
    split = own_x.shape[1]
    total = own_x[...] + got_x[...].astype(jnp.float32)
    out_ref[:, :split] = scale * total + noise_ref[:, :split]
    total = own_y[...]
    for block in got_y:
        total += block[...].astype(jnp.float32)
    out_ref[:, split:] = scale * total + noise_ref[:, split:]


def update_call(scale, parts, noise, after):
    rows, cols = noise.shape
    spec = lambda a: pl.BlockSpec((rows // 3, a.shape[1]), lambda n: (n, 0))
    return pl.pallas_call(
        functools.partial(update_kernel, scale),
        grid=(3,),
        in_specs=[spec(a) for a in parts] + [spec(noise), ANY],
        out_specs=spec(noise),
        out_shape=jax.ShapeDtypeStruct(noise.shape, jnp.float32),
        compiler_params=params(24, "arbitrary"),
        cost_estimate=LITTLE,
        name="update",
    )(*parts, noise, after)


def local(gate_pre, up_pre, out_grad, down_weight, token_user, noise):
    users_group = USR_DEV * NP * NZ
    groups = NX * NY * NC
    clip_bound = 0.5 * math.sqrt(SLOTS * F * D)
    width = D // groups
    rows = gate_pre.shape[0]
    core = lax.axis_index("c")
    x_index = lax.axis_index("x")
    y_index = lax.axis_index("yh")

    weight = down_weight.T
    weight_other = lax.ppermute(weight, "yh", shift(NY, 1))
    pair = lax.axis_index("yl")
    ring = lax.axis_index("z")
    other = lax.ppermute(out_grad, "yl", shift(NP, 1))
    left = lax.ppermute(out_grad, "z", shift(NZ, 1))
    right = lax.ppermute(out_grad, "z", shift(NZ, -1))
    far = lax.ppermute(out_grad, "z", shift(NZ, 2))

    hidden = hidden_call(gate_pre, up_pre)
    other, left, right, far, hidden, weight_other = lax.optimization_barrier(
        (other, left, right, far, hidden, weight_other)
    )
    weights = [
        lax.all_gather(part, ("x", "c"), axis=0, tiled=True) for part in (weight, weight_other)
    ]
    other_left = lax.ppermute(other, "z", shift(NZ, 1))
    other_right = lax.ppermute(other, "z", shift(NZ, -1))
    other_far = lax.ppermute(far, "yl", shift(NP, 1))

    hidden_sib = lax.ppermute(hidden, "c", shift(NC, 1))
    user_row = token_user.reshape(1, rows)
    user_sib = lax.ppermute(user_row, "c", shift(NC, 1))
    gram = hidden_gram_call(hidden, token_user, user_row)

    other_left, other_right, other_far, user_sib, gram = lax.optimization_barrier(
        (other_left, other_right, other_far, user_sib, gram)
    )
    pieces = [out_grad, left, right, far, other, other_left, other_right, other_far]
    place = [
        (at * NZ + (ring + step) % NZ) * out_grad.shape[0]
        for at in (pair, 1 - pair)
        for step in (0, 3, 1, 2)
    ]
    place = jnp.stack([core, x_index, y_index, *place]).astype(jnp.int32)
    grad_rows, squares = grad_gram_call(place, pieces, gram, user_row, users_group)
    mine, others = transpose_call(place, grad_rows, width)
    squares_sib = lax.ppermute(squares, "c", shift(NC, 1))
    squares_sib, others = lax.optimization_barrier((squares_sib, others))
    theirs = lax.ppermute(others, "c", shift(NC, 1))
    squares = jnp.concatenate([squares, squares_sib], axis=0)
    squares = squares + lax.ppermute(squares, "yl", shift(NP, 1))
    squares = squares + lax.ppermute(squares, "z", [(0, 1), (1, 0), (2, 3), (3, 2)])
    more = lax.ppermute(squares, "z", [(0, 3), (3, 0), (1, 2), (2, 1)])

    cols = hidden.shape[1]
    split = (cols // TILE + 1) // 2 * TILE
    term = lambda by_x, start, count, after: term_call(
        by_x, place, mine, theirs, hidden, hidden_sib, squares, more, user_row, user_sib,
        clip_bound, start, count, after,
    )
    *term_x, done = term(True, 0, split, place)
    got_x = {dx: lax.ppermute(term_x[dx], "x", shift(NX, dx)) for dx in (2, 1, 3)}
    *term_y, done = term(False, split, cols - split, done)
    got_y = [lax.ppermute(part, "yh", shift(NY, 1)) for part in term_y[2:]]

    steps = cols // TILE
    early = (2 * steps) // 3
    *held, done = grads_call(place, grad_rows, weights, gate_pre, up_pre, done, 0, early, ())

    keep_x, send_x = add_call(
        add_x_kernel, [term_x[0], *got_x.values()], width, 1, (done,)
    )
    last_x = lax.ppermute(send_x, "yh", shift(NY, 1))
    keep_y, *send_y = add_call(add_y_kernel, [*term_y[:2], *got_y], width, NX - 1, (done,))
    last_y = [lax.ppermute(send_y[dx - 1], "x", shift(NX, dx)) for dx in (2, 1, 3)]

    gate_grad, up_grad, done = grads_call(
        place, grad_rows, weights, gate_pre, up_pre, send_y[0], early, steps - early, held
    )
    scale = math.sqrt(F * D) / (users_group * groups * clip_bound)
    weight_update = update_call(
        scale, [keep_x, last_x, keep_y, *last_y], noise.T, done
    ).T
    return (gate_grad, up_grad, weight_update)


def solution(mesh):
    fine = Mesh(mesh.devices.reshape(NX, NY, NC, NP, NZ), ("x", "yh", "c", "yl", "z"))
    fsdp = ("x", "yh", "c")
    user = ("yl", "z")
    return jax.shard_map(
        local,
        mesh=fine,
        in_specs=(
            P(fsdp, user),
            P(fsdp, user),
            P(fsdp + user, None),
            P(user, fsdp),
            P(fsdp, None),
            P(user, fsdp),
        ),
        out_specs=(P(fsdp, user), P(fsdp, user), P(user, fsdp)),
        check_vma=False,
    )
```

time: 366 us -> 164 us (0.45)
  waiting for transfers between devices: 208 us -> 38.2 us
  Pallas kernels: 0 us -> 66.9 us
  matrix products: 64.7 us -> 0 us
  local copies, waits for them, and re-layouts: 51.5 us -> 12.9 us
  starting transfers between devices: 0.11 us -> 30.4 us
  blocking collectives: 18.9 us -> 0 us
  other arithmetic: 9.12 us -> 0.01 us
    reduce_scatter x1 -> x0, waiting for transfers between devices: 109 us -> none  [local(): lax.psum_scatter(lax.dot_general(columns, hidden, (((0,), (0,)), ((), ())...]
    all_gather x2, waiting for transfers between devices: 97.2 us -> 0.01 us  [local(): lax.all_gather(part, ('x', 'c'), axis=0, tiled=True)]
    pallas_call x0 -> x11, Pallas kernels: none -> 66.9 us  [the longest x2 26.3 us: grads_call(): pl.pallas_call(grads_kernel, grid=(steps,), in_specs=[SMEM, pl.BlockSpec(...]
    dot_general x4 -> x0, matrix products: 64.7 us -> none  [the longest x1 27.7 us: local(): lax.dot_general(columns, lax.all_gather(down_weight, 'fsdp', axis=1, tile...]
    gather x2 -> x0, local copies, waits for them, and re-layouts: 42.6 us -> none  [slot_gram(): gathered = jnp.take(values, slot_rows, axis=0) * slot_mask]
    ppermute x0 -> x24, waiting for transfers between devices: none -> 37.6 us  [the longest x1 11.9 us: local(): right = lax.ppermute(out_grad, 'z', shift(NZ, -1))]
    ppermute x0 -> x24, starting transfers between devices: none -> 30.3 us  [the longest x3 6.34 us: local(): lax.ppermute(term_x[dx], 'x', shift(NX, dx))]
    psum x1 -> x0, blocking collectives: 18.9 us -> none  [local(): squares = lax.psum(partial_squares, 'user')]
  transfers between devices with their start and end apart: 3 -> 26, of which waited for: 3 -> 9; matrix products, arithmetic and copies ran while one was open for 13% -> 0% of each run, Pallas kernels for 0% -> 40%
where the time goes in v1:
time: 164 us; the launch traced here: 163 us
  Pallas kernels  66.9 us (41%)
  waiting for transfers between devices  38.2 us (23%)
  starting transfers between devices  30.4 us (19%)
  between operations  14.4 us (9%)
  local copies, waits for them, and re-layouts  12.9 us (8%)
    pallas_call x2, Pallas kernels, grads_call(): pl.pallas_call(grads_kernel, grid=(steps,), in_specs=[SMEM, pl.BlockSpec(...  26.3 us
    pallas_call x2, Pallas kernels, term_call(): pl.pallas_call(functools.partial(term_kernel, clip_bound, by_x), grid=(co...  18.5 us
    unnamed x38, local copies, waits for them, and re-layouts  12.8 us
    ppermute x1, waiting for transfers between devices, local(): right = lax.ppermute(out_grad, 'z', shift(NZ, -1))  11.9 us
    ppermute x1, waiting for transfers between devices, local(): other_far = lax.ppermute(far, 'yl', shift(NP, 1))  7.04 us
    ppermute x3, starting transfers between devices, local(): lax.ppermute(term_x[dx], 'x', shift(NX, dx))  6.34 us
    pallas_call x1, Pallas kernels, grad_gram_call(): pl.pallas_call(grad_gram_kernel, in_specs=[SMEM] + [ANY] * len(pieces) +...  5.97 us
    pallas_call x2, Pallas kernels, add_call(): pl.pallas_call(kernel, grid=(2,), in_specs=[tile(a.shape[0]) for a in par...  5.28 us
  transfers between devices with their start and end apart: 26, of which 9 were waited for; matrix products, arithmetic and copies ran while one was open for 0% of the time, Pallas kernels for 40%

profile of v1, /device:TPU:0, one launch (start us, length us, event | category | flops | bytes accessed | tf_op | source)
XLA Modules:
  0.0 162.7 jit_solution(2423762812702212547)
XLA Ops:
  7.9 3.4 %collective-permute-start.4 = (bf16[144,2304]{1,0:T(8,128)(2,1)}, bf16[144,2304]{1,0:T(8,128)(2,1)}, u32[]{:S(2)}, u32[]{:S(2)}) collective-permute-start(bf16[144,2304]{1,0:T(8,128)(2,1)} %bitcast.25), channel_id=1, source_target_pairs={{0,16},{16,0},{1,17},{17,1},{2,18},{18,2},{3,19},{19,3},{4,20},{20... | collective-permute-start | bytes 1990664 | tf_op jit(solution)/shard_map/ppermute | solution.py:359
  11.3 4.0 %collective-permute-start.2 = (bf16[128,2304]{1,0:T(8,128)(2,1)}, bf16[128,2304]{1,0:T(8,128)(2,1)S(1)}, u32[]{:S(2)}, u32[]{:S(2)}) collective-permute-start(bf16[128,2304]{1,0:T(8,128)(2,1)} %refs_0_.1), channel_id=1, source_target_pairs={{0,3},{1,0},{2,1},{3,2},{4,7},{5,4},{6,5},{7,6},{8,11},{9,8},{10,9... | collective-permute-start | bytes 1769480 | tf_op jit(solution)/shard_map/ppermute | solution.py:364
  17.9 2.3 %copy-done.2 = bf16[1024,2304]{1,0:T(8,128)(2,1)S(1)} copy-done((bf16[1024,2304]{1,0:T(8,128)(2,1)S(1)}, bf16[1024,2304]{1,0:T(8,128)(2,1)}, u32[]{:S(2)}) %copy-start.2) | copy-done | bytes 4718616
  20.2 2.7 %copy-done.3 = bf16[1024,2304]{1,0:T(8,128)(2,1)S(1)} copy-done((bf16[1024,2304]{1,0:T(8,128)(2,1)S(1)}, bf16[1024,2304]{1,0:T(8,128)(2,1)}, u32[]{:S(2)}) %copy-start.3) | copy-done | bytes 4718616
  22.9 3.6 %hidden.1.hidden_ref.own_ref = bf16[1024,2304]{1,0:T(8,128)(2,1)S(1)} custom-call(bf16[1024,2304]{1,0:T(8,128)(2,1)S(1)} %copy-done.2, bf16[1024,2304]{1,0:T(8,128)(2,1)S(1)} %copy-done.3), custom_call_target="tpu_custom_call" | custom-call | flops 1 | bytes 1 | tf_op jit(solution)/shard_map/hidden/pallas_call | solution.py:57
  28.8 11.9 %collective-permute-done.2.refs_2_ = bf16[128,2304]{1,0:T(8,128)(2,1)S(1)} collective-permute-done((bf16[128,2304]{1,0:T(8,128)(2,1)}, bf16[128,2304]{1,0:T(8,128)(2,1)S(1)}, u32[]{:S(2)}, u32[]{:S(2)}) %collective-permute-start.2) | collective-permute-done | bytes 589856 | tf_op jit(solution)/shard_map/ppermute | solution.py:364
  40.6 3.3 %collective-permute-done.1.refs_1_ = bf16[128,2304]{1,0:T(8,128)(2,1)S(1)} collective-permute-done((bf16[128,2304]{1,0:T(8,128)(2,1)}, bf16[128,2304]{1,0:T(8,128)(2,1)S(1)}, u32[]{:S(2)}, u32[]{:S(2)}) %collective-permute-start.1) | collective-permute-done | bytes 589856 | tf_op jit(solution)/shard_map/ppermute | solution.py:363
  47.2 2.4 %copy-done.1 = bf16[1024,2304]{1,0:T(8,128)(2,1)S(1)} copy-done((bf16[1024,2304]{1,0:T(8,128)(2,1)S(1)}, bf16[1024,2304]{1,0:T(8,128)(2,1)}, u32[]{:S(2)}) %copy-start.1) | copy-done | bytes 4718616
  49.6 3.2 %hidden_gram.1.refs_8_ = f32[10,256,256]{2,1,0:T(8,128)S(1)} custom-call(bf16[1024,2304]{1,0:T(8,128)(2,1)S(1)} %copy-done.1, s32[1024,1]{1,0:T(8,128)S(1)} %copy.11.user_ref, s32[1,1024]{1,0:T(1,128)S(1)} %bitcast.19), custom_call_target="tpu_custom_call" | custom-call | flops 1 | bytes 1 | tf_op jit(solution)/shard_map/hidden_gram/pallas_call | solution.py:91
  52.8 7.0 %collective-permute-done.7.refs_7_ = bf16[128,2304]{1,0:T(8,128)(2,1)} collective-permute-done((bf16[128,2304]{1,0:T(8,128)(2,1)S(1)}, bf16[128,2304]{1,0:T(8,128)(2,1)}, u32[]{:S(2)}, u32[]{:S(2)}) %collective-permute-start.7) | collective-permute-done | bytes 589856 | tf_op jit(solution)/shard_map/ppermute | solution.py:376
  61.5 6.0 %grad_gram.1 = (bf16[1024,2304]{1,0:T(8,128)(2,1)S(1)}, f32[16,128]{1,0:T(8,128)S(1)}) custom-call(s32[11]{0:T(128)S(1)} %stack.47.place_ref.after_ref, bf16[128,2304]{1,0:T(8,128)(2,1)S(1)} %copy-done.8, bf16[128,2304]{1,0:T(8,128)(2,1)S(1)} %collective-permute-done.1.refs_1_, bf16[128,2304]{1,0:T(8,128)(2,1)S(1)} %collective-permute-done.2.refs_2_, ...), custom_call_target="tpu_custom_call" | custom-call | flops 1 | bytes 1 | tf_op jit(solution)/shard_map/grad_gram/pallas_call | solution.py:131
  67.6 2.2 %transpose.17 = (bf16[8,144,1024]{2,1,0:T(8,128)(2,1)S(1)}, bf16[8,144,1024]{2,1,0:T(8,128)(2,1)S(1)}) custom-call(s32[11]{0:T(128)S(1)} %stack.47.place_ref.after_ref, bf16[1024,2304]{1,0:T(8,128)(2,1)S(1)} %get-tuple-element.51.grad_ref), custom_call_target="tpu_custom_call" | custom-call | flops 1 | bytes 1 | tf_op jit(solution)/shard_map/transpose/pallas_call | solution.py:160
  71.8 2.3 %collective-permute-done.12 = f32[32,128]{1,0:T(8,128)S(1)} collective-permute-done((f32[32,128]{1,0:T(8,128)S(1)}, f32[32,128]{1,0:T(8,128)S(1)}, u32[]{:S(2)}, u32[]{:S(2)}) %collective-permute-start.12) | collective-permute-done | bytes 16416 | tf_op jit(solution)/shard_map/ppermute | solution.py:399
  75.1 2.8 %collective-permute-done.13 = f32[32,128]{1,0:T(8,128)S(1)} collective-permute-done((f32[32,128]{1,0:T(8,128)S(1)}, f32[32,128]{1,0:T(8,128)S(1)}, u32[]{:S(2)}, u32[]{:S(2)}) %collective-permute-start.13) | collective-permute-done | bytes 16416 | tf_op jit(solution)/shard_map/ppermute | solution.py:400
  78.3 4.5 %collective-permute-done.14.more_ref = f32[32,128]{1,0:T(8,128)S(1)} collective-permute-done((f32[32,128]{1,0:T(8,128)S(1)}, f32[32,128]{1,0:T(8,128)S(1)}, u32[]{:S(2)}, u32[]{:S(2)}) %collective-permute-start.14) | collective-permute-done | bytes 16416 | tf_op jit(solution)/shard_map/ppermute | solution.py:401
  82.9 9.9 %term_x.1 = (bf16[288,1280]{1,0:T(8,128)(2,1)S(1)}, bf16[288,1280]{1,0:T(8,128)(2,1)S(1)}, bf16[288,1280]{1,0:T(8,128)(2,1)S(1)}, bf16[288,1280]{1,0:T(8,128)(2,1)S(1)}, f32[8,128]{1,0:T(8,128)S(1)}) custom-call(s32[11]{0:T(128)S(1)} %stack.47.place_ref.after_ref, bf16[8,144,1024]{2,1,0:T(8,128)(2,1)S(1)} %get-tuple-element.53.mine_ref, ...), custom_call_target="tpu_custom_call" | custom-call | flops 1 | bytes 1 | tf_op jit(solution)/shard_map/term_x/pallas_call | solution.py:228
  92.9 3.1 %collective-permute-start.17 = (bf16[288,1280]{1,0:T(8,128)(2,1)S(1)}, bf16[288,1280]{1,0:T(8,128)(2,1)}, u32[]{:S(2)}, u32[]{:S(2)}) collective-permute-start(bf16[288,1280]{1,0:T(8,128)(2,1)S(1)} %get-tuple-element.72), channel_id=1, source_target_pairs={{0,64},{32,96},{64,0},{96,32},{1,65},{33,97},{65,1},{97,33},{2,66}... | collective-permute-start | bytes 2211848 | tf_op jit(solution)/shard_map/ppermute | solution.py:410
  96.6 2.6 %collective-permute-start.19 = (bf16[288,1280]{1,0:T(8,128)(2,1)S(1)}, bf16[288,1280]{1,0:T(8,128)(2,1)}, u32[]{:S(2)}, u32[]{:S(2)}) collective-permute-start(bf16[288,1280]{1,0:T(8,128)(2,1)S(1)} %get-tuple-element.74), channel_id=1, source_target_pairs={{0,96},{32,0},{64,32},{96,64},{1,97},{33,1},{65,33},{97,65},{2,98}... | collective-permute-start | bytes 2211848 | tf_op jit(solution)/shard_map/ppermute | solution.py:410
  99.2 8.5 %term_y.1 = (bf16[288,1024]{1,0:T(8,128)(2,1)S(1)}, bf16[288,1024]{1,0:T(8,128)(2,1)S(1)}, bf16[288,1024]{1,0:T(8,128)(2,1)S(1)}, bf16[288,1024]{1,0:T(8,128)(2,1)S(1)}, f32[8,128]{1,0:T(8,128)S(1)}) custom-call(s32[11]{0:T(128)S(1)} %stack.47.place_ref.after_ref, bf16[8,144,1024]{2,1,0:T(8,128)(2,1)S(1)} %get-tuple-element.53.mine_ref, ...), custom_call_target="tpu_custom_call" | custom-call | flops 1 | bytes 1 | tf_op jit(solution)/shard_map/term_y/pallas_call | solution.py:228
  113.6 15.9 %grads.2 = (bf16[1024,2304]{1,0:T(8,128)(2,1)}, bf16[1024,2304]{1,0:T(8,128)(2,1)}, f32[8,128]{1,0:T(8,128)}) custom-call(s32[11]{0:T(128)} %copy-done.13, bf16[1024,2304]{1,0:T(8,128)(2,1)} %copy-done.4, bf16[1152,2304]{1,0:T(8,128)(2,1)} %all-gather.3.cloned.1.call-done.same_ref, bf16[1152,2304]{1,0:T(8,128)(2,1)} %all-gather.5.cloned.1.call-done.other_ref, ...), custom_call_target="tpu_custom_call" | custom-call | flops 1 | bytes 1 | tf_op jit(solution)/shard_map/grads/pallas_call | solution.py:299
  129.5 2.7 %add.79 = (f32[144,1280]{1,0:T(8,128)}, bf16[144,1280]{1,0:T(8,128)(2,1)}) custom-call(bf16[288,1280]{1,0:T(8,128)(2,1)} %copy-done.7, bf16[288,1280]{1,0:T(8,128)(2,1)} %collective-permute-done.17.refs_1_, bf16[288,1280]{1,0:T(8,128)(2,1)} %collective-permute-done.18.refs_2_, bf16[288,1280]{1,0:T(8,128)(2,1)} %collective-permute-done.19.refs_3_, ...), custom_call_target="tpu_custom_call" | custom-call | flops 1 | bytes 1 | tf_op jit(solution)/shard_map/add/pallas_call | solution.py:263
  134.4 4.0 %collective-permute-done.16.second_high = bf16[288,1024]{1,0:T(8,128)(2,1)} collective-permute-done((bf16[288,1024]{1,0:T(8,128)(2,1)S(1)}, bf16[288,1024]{1,0:T(8,128)(2,1)}, u32[]{:S(2)}, u32[]{:S(2)}) %collective-permute-start.16) | collective-permute-done | bytes 589856 | tf_op jit(solution)/shard_map/ppermute | solution.py:412
  138.4 2.5 %add.78 = (f32[144,1024]{1,0:T(8,128)}, bf16[144,1024]{1,0:T(8,128)(2,1)}, bf16[144,1024]{1,0:T(8,128)(2,1)}, bf16[144,1024]{1,0:T(8,128)(2,1)}) custom-call(bf16[288,1024]{1,0:T(8,128)(2,1)} %copy-done.10, bf16[288,1024]{1,0:T(8,128)(2,1)} %copy-done.11, bf16[288,1024]{1,0:T(8,128)(2,1)} %collective-permute-done.15.second_low, ...), custom_call_target="tpu_custom_call" | custom-call | flops 1 | bytes 1 | tf_op jit(solution)/shard_map/add/pallas_call | solution.py:263
  143.0 10.4 %grads.3 = (bf16[1024,2304]{1,0:T(8,128)(2,1)}, bf16[1024,2304]{1,0:T(8,128)(2,1)}, f32[8,128]{1,0:T(8,128)}) custom-call(s32[11]{0:T(128)} %copy-done.13, bf16[1024,2304]{1,0:T(8,128)(2,1)} %copy-done.4, bf16[1152,2304]{1,0:T(8,128)(2,1)} %all-gather.3.cloned.1.call-done.same_ref, ...), custom_call_target="tpu_custom_call", output_to_operand_aliasing={{0}: (7, {}), {1}: (8, {})} | custom-call | flops 1 | bytes 1 | tf_op jit(solution)/shard_map/grads/pallas_call | solution.py:299
  (84 shorter events, 26.7 us)
Async XLA Ops:
  7.2 106.4 %all-gather.3.cloned.1.call-start = ((), (), s32[]{:S(2)}) async-start(), calls=%async_computation | async-start | bytes 5971968 | tf_op jit(solution)/shard_map/all_gather | solution.py:372
  7.9 105.7 %all-gather.5.cloned.1.call-start = ((), (), s32[]{:S(2)}) async-start(), calls=%async_computation.1 | async-start | bytes 5971968 | tf_op jit(solution)/shard_map/all_gather | solution.py:372
  7.9 36.0 %collective-permute-start.4 = (bf16[144,2304]{1,0:T(8,128)(2,1)}, bf16[144,2304]{1,0:T(8,128)(2,1)}, u32[]{:S(2)}, u32[]{:S(2)}) collective-permute-start(bf16[144,2304]{1,0:T(8,128)(2,1)} %bitcast.25), channel_id=1, source_target_pairs={{0,16},{16,0},{1,17},{17,1},{2,18},{18,2},{3,19},{19,3},{4,20},{20... | collective-permute-start | bytes 1990664 | tf_op jit(solution)/shard_map/ppermute | solution.py:359
  11.3 29.3 %collective-permute-start.2 = (bf16[128,2304]{1,0:T(8,128)(2,1)}, bf16[128,2304]{1,0:T(8,128)(2,1)S(1)}, u32[]{:S(2)}, u32[]{:S(2)}) collective-permute-start(bf16[128,2304]{1,0:T(8,128)(2,1)} %refs_0_.1), channel_id=1, source_target_pairs={{0,3},{1,0},{2,1},{3,2},{4,7},{5,4},{6,5},{7,6},{8,11},{9,8},{10,9... | collective-permute-start | bytes 1769480 | tf_op jit(solution)/shard_map/ppermute | solution.py:364
  15.3 28.6 %collective-permute-start.1 = (bf16[128,2304]{1,0:T(8,128)(2,1)}, bf16[128,2304]{1,0:T(8,128)(2,1)S(1)}, u32[]{:S(2)}, u32[]{:S(2)}) collective-permute-start(bf16[128,2304]{1,0:T(8,128)(2,1)} %refs_0_.1), channel_id=1, source_target_pairs={{0,1},{1,2},{2,3},{3,0},{4,5},{5,6},{6,7},{7,4},{8,9},{9,10},{10,1... | collective-permute-start | bytes 1769480 | tf_op jit(solution)/shard_map/ppermute | solution.py:363
  15.3 28.6 %collective-permute-start = (bf16[128,2304]{1,0:T(8,128)(2,1)}, bf16[128,2304]{1,0:T(8,128)(2,1)S(1)}, u32[]{:S(2)}, u32[]{:S(2)}) collective-permute-start(bf16[128,2304]{1,0:T(8,128)(2,1)} %refs_0_.1), channel_id=1, source_target_pairs={{0,4},{4,0},{1,5},{5,1},{2,6},{6,2},{3,7},{7,3},{8,12},{12,8},{9,1... | collective-permute-start | bytes 1769480 | tf_op jit(solution)/shard_map/ppermute | solution.py:362
  16.0 27.9 %collective-permute-start.3 = (bf16[128,2304]{1,0:T(8,128)(2,1)}, bf16[128,2304]{1,0:T(8,128)(2,1)S(1)}, u32[]{:S(2)}, u32[]{:S(2)}) collective-permute-start(bf16[128,2304]{1,0:T(8,128)(2,1)} %refs_0_.1), channel_id=1, source_target_pairs={{0,2},{1,3},{2,0},{3,1},{4,6},{5,7},{6,4},{7,5},{8,10},{9,11},{10,... | collective-permute-start | bytes 1769480 | tf_op jit(solution)/shard_map/ppermute | solution.py:365
  43.9 38.9 %collective-permute-start.11 = (bf16[1024,2304]{1,0:T(8,128)(2,1)}, bf16[1024,2304]{1,0:T(8,128)(2,1)}, u32[]{:S(2)}, u32[]{:S(2)}) collective-permute-start(bf16[1024,2304]{1,0:T(8,128)(2,1)} %copy-done), channel_id=1, source_target_pairs={{0,8},{8,0},{1,9},{9,1},{2,10},{10,2},{3,11},{11,3},{4,12},{12,4},... | collective-permute-start | bytes 14155784 | tf_op jit(solution)/shard_map/ppermute | solution.py:378
  44.0 15.8 %collective-permute-start.7 = (bf16[128,2304]{1,0:T(8,128)(2,1)S(1)}, bf16[128,2304]{1,0:T(8,128)(2,1)}, u32[]{:S(2)}, u32[]{:S(2)}) collective-permute-start(bf16[128,2304]{1,0:T(8,128)(2,1)S(1)} %collective-permute-done.3.refs_3_), channel_id=1, source_target_pairs={{0,4},{4,0},{1,5},{5,1},{2,6},{6,2},{3,7},{7,3},{8,12},{12,8},{9,1... | collective-permute-start | bytes 1769480 | tf_op jit(solution)/shard_map/ppermute | solution.py:376
  44.8 15.5 %collective-permute-start.6 = (bf16[128,2304]{1,0:T(8,128)(2,1)S(1)}, bf16[128,2304]{1,0:T(8,128)(2,1)}, u32[]{:S(2)}, u32[]{:S(2)}) collective-permute-start(bf16[128,2304]{1,0:T(8,128)(2,1)S(1)} %collective-permute-done.refs_4_), channel_id=1, source_target_pairs={{0,3},{1,0},{2,1},{3,2},{4,7},{5,4},{6,5},{7,6},{8,11},{9,8},{10,9... | collective-permute-start | bytes 1769480 | tf_op jit(solution)/shard_map/ppermute | solution.py:375
  45.1 16.4 %collective-permute-start.5 = (bf16[128,2304]{1,0:T(8,128)(2,1)S(1)}, bf16[128,2304]{1,0:T(8,128)(2,1)}, u32[]{:S(2)}, u32[]{:S(2)}) collective-permute-start(bf16[128,2304]{1,0:T(8,128)(2,1)S(1)} %collective-permute-done.refs_4_), channel_id=1, source_target_pairs={{0,1},{1,2},{2,3},{3,0},{4,5},{5,6},{6,7},{7,4},{8,9},{9,10},{10,1... | collective-permute-start | bytes 1769480 | tf_op jit(solution)/shard_map/ppermute | solution.py:374
  46.8 6.0 %collective-permute-start.8 = (s32[1,1024]{1,0:T(1,128)S(1)}, s32[1,1024]{1,0:T(1,128)S(1)}, u32[]{:S(2)}, u32[]{:S(2)}) collective-permute-start(s32[1,1024]{1,0:T(1,128)S(1)} %bitcast.18), channel_id=1, source_target_pairs={{0,8},{8,0},{1,9},{9,1},{2,10},{10,2},{3,11},{11,3},{4,12},{12,4},... | collective-permute-start | bytes 12296 | tf_op jit(solution)/shard_map/ppermute | solution.py:380
  69.9 13.0 %collective-permute-start.10 = (bf16[8,144,1024]{2,1,0:T(8,128)(2,1)S(1)}, bf16[8,144,1024]{2,1,0:T(8,128)(2,1)S(1)}, u32[]{:S(2)}, u32[]{:S(2)}) collective-permute-start(bf16[8,144,1024]{2,1,0:T(8,128)(2,1)S(1)} %get-tuple-element.56), channel_id=1, source_target_pairs={{0,8},{8,0},{1,9},{9,1},{2,10},{10,2},{3,11},{11,3},{4,12},{12,4},... | collective-permute-start | bytes 7077896 | tf_op jit(solution)/shard_map/ppermute | solution.py:397
  70.4 3.7 %collective-permute-start.12 = (f32[32,128]{1,0:T(8,128)S(1)}, f32[32,128]{1,0:T(8,128)S(1)}, u32[]{:S(2)}, u32[]{:S(2)}) collective-permute-start(f32[32,128]{1,0:T(8,128)S(1)} %constant_dynamic-update-slice_fusion), channel_id=1, source_target_pairs={{0,4},{4,0},{1,5},{5,1},{2,6},{6,2},{3,7},{7,3},{8,12},{12,8},{9,1... | collective-permute-start | bytes 49160 | tf_op jit(solution)/shard_map/ppermute | solution.py:399
  77.9 5.0 %collective-permute-start.14 = (f32[32,128]{1,0:T(8,128)S(1)}, f32[32,128]{1,0:T(8,128)S(1)}, u32[]{:S(2)}, u32[]{:S(2)}) collective-permute-start(f32[32,128]{1,0:T(8,128)S(1)} %add.77.squares_ref), channel_id=1, source_target_pairs={{0,3},{3,0},{1,2},{2,1},{4,7},{7,4},{5,6},{6,5},{8,11},{11,8},{9,1... | collective-permute-start | bytes 49160 | tf_op jit(solution)/shard_map/ppermute | solution.py:401
  92.9 36.6 %collective-permute-start.17 = (bf16[288,1280]{1,0:T(8,128)(2,1)S(1)}, bf16[288,1280]{1,0:T(8,128)(2,1)}, u32[]{:S(2)}, u32[]{:S(2)}) collective-permute-start(bf16[288,1280]{1,0:T(8,128)(2,1)S(1)} %get-tuple-element.72), channel_id=1, source_target_pairs={{0,64},{32,96},{64,0},{96,32},{1,65},{33,97},{65,1},{97,33},{2,66}... | collective-permute-start | bytes 2211848 | tf_op jit(solution)/shard_map/ppermute | solution.py:410
  96.0 33.5 %collective-permute-start.18 = (bf16[288,1280]{1,0:T(8,128)(2,1)S(1)}, bf16[288,1280]{1,0:T(8,128)(2,1)}, u32[]{:S(2)}, u32[]{:S(2)}) collective-permute-start(bf16[288,1280]{1,0:T(8,128)(2,1)S(1)} %get-tuple-element.73), channel_id=1, source_target_pairs={{0,32},{32,64},{64,96},{96,0},{1,33},{33,65},{65,97},{97,1},{2,34}... | collective-permute-start | bytes 2211848 | tf_op jit(solution)/shard_map/ppermute | solution.py:410
  96.6 32.9 %collective-permute-start.19 = (bf16[288,1280]{1,0:T(8,128)(2,1)S(1)}, bf16[288,1280]{1,0:T(8,128)(2,1)}, u32[]{:S(2)}, u32[]{:S(2)}) collective-permute-start(bf16[288,1280]{1,0:T(8,128)(2,1)S(1)} %get-tuple-element.74), channel_id=1, source_target_pairs={{0,96},{32,0},{64,32},{96,64},{1,97},{33,1},{65,33},{97,65},{2,98}... | collective-permute-start | bytes 2211848 | tf_op jit(solution)/shard_map/ppermute | solution.py:410
  110.0 24.4 %collective-permute-start.15 = (bf16[288,1024]{1,0:T(8,128)(2,1)S(1)}, bf16[288,1024]{1,0:T(8,128)(2,1)}, u32[]{:S(2)}, u32[]{:S(2)}) collective-permute-start(bf16[288,1024]{1,0:T(8,128)(2,1)S(1)} %get-tuple-element.62), channel_id=1, source_target_pairs={{0,16},{16,0},{1,17},{17,1},{2,18},{18,2},{3,19},{19,3},{4,20},{20... | collective-permute-start | bytes 1769480 | tf_op jit(solution)/shard_map/ppermute | solution.py:412
  112.2 26.2 %collective-permute-start.16 = (bf16[288,1024]{1,0:T(8,128)(2,1)S(1)}, bf16[288,1024]{1,0:T(8,128)(2,1)}, u32[]{:S(2)}, u32[]{:S(2)}) collective-permute-start(bf16[288,1024]{1,0:T(8,128)(2,1)S(1)} %get-tuple-element.63), channel_id=1, source_target_pairs={{0,16},{16,0},{1,17},{17,1},{2,18},{18,2},{3,19},{19,3},{4,20},{20... | collective-permute-start | bytes 1769480 | tf_op jit(solution)/shard_map/ppermute | solution.py:412
  132.3 21.2 %collective-permute-start.20 = (bf16[144,1280]{1,0:T(8,128)(2,1)}, bf16[144,1280]{1,0:T(8,128)(2,1)S(1)}, u32[]{:S(2)}, u32[]{:S(2)}) collective-permute-start(bf16[144,1280]{1,0:T(8,128)(2,1)} %get-tuple-element.76), channel_id=1, source_target_pairs={{0,16},{16,0},{1,17},{17,1},{2,18},{18,2},{3,19},{19,3},{4,20},{20... | collective-permute-start | bytes 1105928 | tf_op jit(solution)/shard_map/ppermute | solution.py:421
  140.9 12.5 %collective-permute-start.21 = (bf16[144,1024]{1,0:T(8,128)(2,1)}, bf16[144,1024]{1,0:T(8,128)(2,1)S(1)}, u32[]{:S(2)}, u32[]{:S(2)}) collective-permute-start(bf16[144,1024]{1,0:T(8,128)(2,1)} %get-tuple-element.78), channel_id=1, source_target_pairs={{0,64},{32,96},{64,0},{96,32},{1,65},{33,97},{65,1},{97,33},{2,66}... | collective-permute-start | bytes 884744 | tf_op jit(solution)/shard_map/ppermute | solution.py:423
  140.9 12.5 %collective-permute-start.23 = (bf16[144,1024]{1,0:T(8,128)(2,1)}, bf16[144,1024]{1,0:T(8,128)(2,1)S(1)}, u32[]{:S(2)}, u32[]{:S(2)}) collective-permute-start(bf16[144,1024]{1,0:T(8,128)(2,1)} %get-tuple-element.79), channel_id=1, source_target_pairs={{0,96},{32,0},{64,32},{96,64},{1,97},{33,1},{65,33},{97,65},{2,98}... | collective-permute-start | bytes 884744 | tf_op jit(solution)/shard_map/ppermute | solution.py:423
  142.1 11.4 %collective-permute-start.22 = (bf16[144,1024]{1,0:T(8,128)(2,1)}, bf16[144,1024]{1,0:T(8,128)(2,1)S(1)}, u32[]{:S(2)}, u32[]{:S(2)}) collective-permute-start(bf16[144,1024]{1,0:T(8,128)(2,1)} %get-tuple-element.66.refs_0_), channel_id=1, source_target_pairs={{0,32},{32,64},{64,96},{96,0},{1,33},{33,65},{65,97},{97,1},{2,34}... | collective-permute-start | bytes 884744 | tf_op jit(solution)/shard_map/ppermute | solution.py:423
  (20 other events, 275.6 us)
Sparse Core Ops, SparseCore 0:
  9.7 42.8 all-gather.2
  54.2 33.8 all-gather.4

commit v2 on v1

--- a/solution.py
+++ b/solution.py
@@ -169,25 +169,39 @@
     )(place, grad)
 
 
-def scale_rows(
-    clip_bound, place_ref, mine_ref, theirs_ref, squares_ref, more_ref, user_refs, scaled_ref
+def scaled_tile(
+    clip_bound, place_ref, mine_ref, theirs_ref, squares_ref, more_ref, user_refs, hidden_refs,
+    scaled_ref
 ):
     width, rows = mine_ref.shape[1:]
     count = squares_ref.shape[0] // 2
     ids = lax.broadcasted_iota(jnp.int32, (count, rows), 0)
     x_index, y_index = place_ref[1], place_ref[2]
+    total = None
     for group, ref in enumerate((mine_ref, theirs_ref)):
         inside = pl.ds(group * count, count)
         squares = squares_ref[inside, 0:1] + more_ref[inside, 0:1]
         factor = clip_bound / jnp.maximum(jnp.sqrt(squares), clip_bound)
         chosen = jnp.where(ids == user_refs[group][...], factor, 0.0)
         row_factor = jnp.sum(chosen, axis=0, keepdims=True)
-        for dx in range(NX):
-            for dy in range(NY):
-                block = ref[((x_index + dx) % NX) * NY + (y_index + dy) % NY]
-                scaled_ref[
-                    pl.ds((dx * NY + dy) * width, width), pl.ds(group * rows, rows)
-                ] = (block.astype(jnp.float32) * row_factor).astype(jnp.bfloat16)
+        for start in range(0, rows, 2 * TILE):
+            parts = []
+            for dx in range(NX):
+                for dy in range(NY):
+                    index = ((x_index + dx) % NX) * NY + (y_index + dy) % NY
+                    block = ref[index, :, start : start + 2 * TILE].astype(jnp.float32)
+                    parts.append(
+                        (block * row_factor[:, start : start + 2 * TILE]).astype(jnp.bfloat16)
+                    )
+            scaled = jnp.concatenate(parts, axis=0)
+            scaled_ref[:, pl.ds(group * rows + start, 2 * TILE)] = scaled
+            part = jnp.dot(
+                scaled,
+                hidden_refs[group][pl.ds(start, 2 * TILE), :],
+                preferred_element_type=jnp.float32,
+            )
+            total = part if total is None else total + part
+    return total
 
 
 def term_kernel(
@@ -197,22 +211,30 @@
     outs, token_ref, scaled_ref = refs[:-2], refs[-2], refs[-1]
     token_ref[...] = jnp.zeros_like(token_ref)
 
+    rows = own_ref.shape[0]
+
+    def put(total):
+        total = total.astype(jnp.bfloat16)
+        size = mine_ref.shape[1]
+        for dx in range(NX):
+            for dy in range(NY):
+                out, at = (outs[dx], dy) if by_x else (outs[2 * dy + dx // 2], dx % 2)
+                out[pl.ds(at * size, size), :] = total[(dx * NY + dy) * size :][:size]
+
     @pl.when(pl.program_id(0) == 0)
     def _():
-        scale_rows(
-            clip_bound, place_ref, mine_ref, theirs_ref, squares_ref, more_ref,
-            (user_ref, user_sib_ref), scaled_ref,
+        put(
+            scaled_tile(
+                clip_bound, place_ref, mine_ref, theirs_ref, squares_ref, more_ref,
+                (user_ref, user_sib_ref), (own_ref, sib_ref), scaled_ref,
+            )
         )
 
-    rows = own_ref.shape[0]
-    total = jnp.dot(scaled_ref[:, :rows], own_ref[...], preferred_element_type=jnp.float32)
-    total += jnp.dot(scaled_ref[:, rows:], sib_ref[...], preferred_element_type=jnp.float32)
-    total = total.astype(jnp.bfloat16)
-    size = mine_ref.shape[1]
-    for dx in range(NX):
-        for dy in range(NY):
-            out, at = (outs[dx], dy) if by_x else (outs[2 * dy + dx // 2], dx % 2)
-            out[pl.ds(at * size, size), :] = total[(dx * NY + dy) * size :][:size]
+    @pl.when(pl.program_id(0) > 0)
+    def _():
+        total = jnp.dot(scaled_ref[:, :rows], own_ref[...], preferred_element_type=jnp.float32)
+        total += jnp.dot(scaled_ref[:, rows:], sib_ref[...], preferred_element_type=jnp.float32)
+        put(total)
 
 
 def term_call(
@@ -313,7 +335,7 @@
         out_shape=[jax.ShapeDtypeStruct((rows, cols), jnp.bfloat16)] * 2 + [TOKEN],
         scratch_shapes=[pltpu.VMEM((depth, TILE), jnp.bfloat16)],
         input_output_aliases={7 + k: k for k in range(len(held))},
-        compiler_params=params(56, "arbitrary"),
+        compiler_params=params(52, "arbitrary"),
         cost_estimate=LITTLE,
         name="grads",
     )(place, grad, *weights, gate, up, after, *held)
@@ -412,7 +434,7 @@
     got_y = [lax.ppermute(part, "yh", shift(NY, 1)) for part in term_y[2:]]
 
     steps = cols // TILE
-    early = (2 * steps) // 3
+    early = (2 * steps) // 3 + 1
     *held, done = grads_call(place, grad_rows, weights, gate_pre, up_pre, done, 0, early, ())
 
     keep_x, send_x = add_call(

time: 164 us -> 159 us (0.970)
  Pallas kernels: 66.9 us -> 64.5 us
  waiting for transfers between devices: 38.2 us -> 36 us
    ppermute x2, waiting for transfers between devices: 3.99 us -> 0.01 us  [local(): got_y = [lax.ppermute(part, 'yh', shift(NY, 1)) for part in term_y[2:]]]
    pallas_call x2, Pallas kernels: 18.5 us -> 16.3 us  [term_call(): pl.pallas_call(functools.partial(term_kernel, clip_bound, by_x), grid=(co...]
    ppermute x3, waiting for transfers between devices: 0.01 us -> 1.74 us  [local(): lax.ppermute(send_y[dx - 1], 'x', shift(NX, dx))]
    unnamed x38 -> x36, local copies, waits for them, and re-layouts: 12.8 us -> 13.1 us
where the time goes in v2:
time: 159 us; the launch traced here: 158 us
  Pallas kernels  64.5 us (41%)
  waiting for transfers between devices  36 us (23%)
  starting transfers between devices  30.4 us (19%)
  between operations  14.3 us (9%)
  local copies, waits for them, and re-layouts  13.2 us (8%)
    pallas_call x2, Pallas kernels, grads_call(): pl.pallas_call(grads_kernel, grid=(steps,), in_specs=[SMEM, pl.BlockSpec(...  26.1 us
    pallas_call x2, Pallas kernels, term_call(): pl.pallas_call(functools.partial(term_kernel, clip_bound, by_x), grid=(co...  16.3 us
    unnamed x36, local copies, waits for them, and re-layouts  13.1 us
    ppermute x1, waiting for transfers between devices, local(): right = lax.ppermute(out_grad, 'z', shift(NZ, -1))  11.9 us
    ppermute x1, waiting for transfers between devices, local(): other_far = lax.ppermute(far, 'yl', shift(NP, 1))  7.05 us
    ppermute x3, starting transfers between devices, local(): lax.ppermute(term_x[dx], 'x', shift(NX, dx))  6.34 us
    pallas_call x1, Pallas kernels, grad_gram_call(): pl.pallas_call(grad_gram_kernel, in_specs=[SMEM] + [ANY] * len(pieces) +...  5.97 us
    pallas_call x2, Pallas kernels, add_call(): pl.pallas_call(kernel, grid=(2,), in_specs=[tile(a.shape[0]) for a in par...  5.28 us
  transfers between devices with their start and end apart: 26, of which 9 were waited for; matrix products, arithmetic and copies ran while one was open for 0% of the time, Pallas kernels for 40%

profile of v2, /device:TPU:0, one launch (start us, length us, event | category | flops | bytes accessed | tf_op | source)
XLA Modules:
  0.0 158.4 jit_solution(4226629351212330136)
XLA Ops:
  7.9 3.4 %collective-permute-start.4 = (bf16[144,2304]{1,0:T(8,128)(2,1)}, bf16[144,2304]{1,0:T(8,128)(2,1)}, u32[]{:S(2)}, u32[]{:S(2)}) collective-permute-start(bf16[144,2304]{1,0:T(8,128)(2,1)} %bitcast.25), channel_id=1, source_target_pairs={{0,16},{16,0},{1,17},{17,1},{2,18},{18,2},{3,19},{19,3},{4,20},{20... | collective-permute-start | bytes 1990664 | tf_op jit(solution)/shard_map/ppermute | solution.py:381
  11.3 4.0 %collective-permute-start.2 = (bf16[128,2304]{1,0:T(8,128)(2,1)}, bf16[128,2304]{1,0:T(8,128)(2,1)S(1)}, u32[]{:S(2)}, u32[]{:S(2)}) collective-permute-start(bf16[128,2304]{1,0:T(8,128)(2,1)} %refs_0_.1), channel_id=1, source_target_pairs={{0,3},{1,0},{2,1},{3,2},{4,7},{5,4},{6,5},{7,6},{8,11},{9,8},{10,9... | collective-permute-start | bytes 1769480 | tf_op jit(solution)/shard_map/ppermute | solution.py:386
  17.9 2.3 %copy-done.2 = bf16[1024,2304]{1,0:T(8,128)(2,1)S(1)} copy-done((bf16[1024,2304]{1,0:T(8,128)(2,1)S(1)}, bf16[1024,2304]{1,0:T(8,128)(2,1)}, u32[]{:S(2)}) %copy-start.2) | copy-done | bytes 4718616
  20.2 2.7 %copy-done.3 = bf16[1024,2304]{1,0:T(8,128)(2,1)S(1)} copy-done((bf16[1024,2304]{1,0:T(8,128)(2,1)S(1)}, bf16[1024,2304]{1,0:T(8,128)(2,1)}, u32[]{:S(2)}) %copy-start.3) | copy-done | bytes 4718616
  22.9 3.6 %hidden.1.hidden_ref.own_ref = bf16[1024,2304]{1,0:T(8,128)(2,1)S(1)} custom-call(bf16[1024,2304]{1,0:T(8,128)(2,1)S(1)} %copy-done.2, bf16[1024,2304]{1,0:T(8,128)(2,1)S(1)} %copy-done.3), custom_call_target="tpu_custom_call" | custom-call | flops 1 | bytes 1 | tf_op jit(solution)/shard_map/hidden/pallas_call | solution.py:57
  26.6 2.2 %copy-done = bf16[1024,2304]{1,0:T(8,128)(2,1)} copy-done((bf16[1024,2304]{1,0:T(8,128)(2,1)}, bf16[1024,2304]{1,0:T(8,128)(2,1)S(1)}, u32[]{:S(2)}) %copy-start) | copy-done | bytes 4718616
  28.8 11.9 %collective-permute-done.2.refs_2_ = bf16[128,2304]{1,0:T(8,128)(2,1)S(1)} collective-permute-done((bf16[128,2304]{1,0:T(8,128)(2,1)}, bf16[128,2304]{1,0:T(8,128)(2,1)S(1)}, u32[]{:S(2)}, u32[]{:S(2)}) %collective-permute-start.2) | collective-permute-done | bytes 589856 | tf_op jit(solution)/shard_map/ppermute | solution.py:386
  40.6 3.3 %collective-permute-done.1.refs_1_ = bf16[128,2304]{1,0:T(8,128)(2,1)S(1)} collective-permute-done((bf16[128,2304]{1,0:T(8,128)(2,1)}, bf16[128,2304]{1,0:T(8,128)(2,1)S(1)}, u32[]{:S(2)}, u32[]{:S(2)}) %collective-permute-start.1) | collective-permute-done | bytes 589856 | tf_op jit(solution)/shard_map/ppermute | solution.py:385
  47.2 2.4 %copy-done.1 = bf16[1024,2304]{1,0:T(8,128)(2,1)S(1)} copy-done((bf16[1024,2304]{1,0:T(8,128)(2,1)S(1)}, bf16[1024,2304]{1,0:T(8,128)(2,1)}, u32[]{:S(2)}) %copy-start.1) | copy-done | bytes 4718616
  49.6 3.2 %hidden_gram.1.refs_8_ = f32[10,256,256]{2,1,0:T(8,128)S(1)} custom-call(bf16[1024,2304]{1,0:T(8,128)(2,1)S(1)} %copy-done.1, s32[1024,1]{1,0:T(8,128)S(1)} %copy.11.user_ref, s32[1,1024]{1,0:T(1,128)S(1)} %bitcast.19), custom_call_target="tpu_custom_call" | custom-call | flops 1 | bytes 1 | tf_op jit(solution)/shard_map/hidden_gram/pallas_call | solution.py:91
  52.8 7.0 %collective-permute-done.7.refs_7_ = bf16[128,2304]{1,0:T(8,128)(2,1)} collective-permute-done((bf16[128,2304]{1,0:T(8,128)(2,1)S(1)}, bf16[128,2304]{1,0:T(8,128)(2,1)}, u32[]{:S(2)}, u32[]{:S(2)}) %collective-permute-start.7) | collective-permute-done | bytes 589856 | tf_op jit(solution)/shard_map/ppermute | solution.py:398
  61.5 6.0 %grad_gram.1 = (bf16[1024,2304]{1,0:T(8,128)(2,1)S(1)}, f32[16,128]{1,0:T(8,128)S(1)}) custom-call(s32[11]{0:T(128)S(1)} %stack.47.place_ref.after_ref, bf16[128,2304]{1,0:T(8,128)(2,1)S(1)} %copy-done.8, bf16[128,2304]{1,0:T(8,128)(2,1)S(1)} %collective-permute-done.1.refs_1_, bf16[128,2304]{1,0:T(8,128)(2,1)S(1)} %collective-permute-done.2.refs_2_, ...), custom_call_target="tpu_custom_call" | custom-call | flops 1 | bytes 1 | tf_op jit(solution)/shard_map/grad_gram/pallas_call | solution.py:131
  67.6 2.2 %transpose.17 = (bf16[8,144,1024]{2,1,0:T(8,128)(2,1)S(1)}, bf16[8,144,1024]{2,1,0:T(8,128)(2,1)S(1)}) custom-call(s32[11]{0:T(128)S(1)} %stack.47.place_ref.after_ref, bf16[1024,2304]{1,0:T(8,128)(2,1)S(1)} %get-tuple-element.51.grad_ref), custom_call_target="tpu_custom_call" | custom-call | flops 1 | bytes 1 | tf_op jit(solution)/shard_map/transpose/pallas_call | solution.py:160
  71.8 2.3 %collective-permute-done.12 = f32[32,128]{1,0:T(8,128)S(1)} collective-permute-done((f32[32,128]{1,0:T(8,128)S(1)}, f32[32,128]{1,0:T(8,128)S(1)}, u32[]{:S(2)}, u32[]{:S(2)}) %collective-permute-start.12) | collective-permute-done | bytes 16416 | tf_op jit(solution)/shard_map/ppermute | solution.py:421
  75.1 2.8 %collective-permute-done.13 = f32[32,128]{1,0:T(8,128)S(1)} collective-permute-done((f32[32,128]{1,0:T(8,128)S(1)}, f32[32,128]{1,0:T(8,128)S(1)}, u32[]{:S(2)}, u32[]{:S(2)}) %collective-permute-start.13) | collective-permute-done | bytes 16416 | tf_op jit(solution)/shard_map/ppermute | solution.py:422
  78.3 4.5 %collective-permute-done.14.more_ref = f32[32,128]{1,0:T(8,128)S(1)} collective-permute-done((f32[32,128]{1,0:T(8,128)S(1)}, f32[32,128]{1,0:T(8,128)S(1)}, u32[]{:S(2)}, u32[]{:S(2)}) %collective-permute-start.14) | collective-permute-done | bytes 16416 | tf_op jit(solution)/shard_map/ppermute | solution.py:423
  82.9 8.9 %term_x.1 = (bf16[288,1280]{1,0:T(8,128)(2,1)S(1)}, bf16[288,1280]{1,0:T(8,128)(2,1)S(1)}, bf16[288,1280]{1,0:T(8,128)(2,1)S(1)}, bf16[288,1280]{1,0:T(8,128)(2,1)S(1)}, f32[8,128]{1,0:T(8,128)S(1)}) custom-call(s32[11]{0:T(128)S(1)} %stack.47.place_ref.after_ref, bf16[8,144,1024]{2,1,0:T(8,128)(2,1)S(1)} %get-tuple-element.53.mine_ref, ...), custom_call_target="tpu_custom_call" | custom-call | flops 1 | bytes 1 | tf_op jit(solution)/shard_map/term_x/pallas_call | solution.py:250
  91.8 3.1 %collective-permute-start.17 = (bf16[288,1280]{1,0:T(8,128)(2,1)S(1)}, bf16[288,1280]{1,0:T(8,128)(2,1)}, u32[]{:S(2)}, u32[]{:S(2)}) collective-permute-start(bf16[288,1280]{1,0:T(8,128)(2,1)S(1)} %get-tuple-element.72), channel_id=1, source_target_pairs={{0,64},{32,96},{64,0},{96,32},{1,65},{33,97},{65,1},{97,33},{2,66}... | collective-permute-start | bytes 2211848 | tf_op jit(solution)/shard_map/ppermute | solution.py:432
  95.5 2.6 %collective-permute-start.19 = (bf16[288,1280]{1,0:T(8,128)(2,1)S(1)}, bf16[288,1280]{1,0:T(8,128)(2,1)}, u32[]{:S(2)}, u32[]{:S(2)}) collective-permute-start(bf16[288,1280]{1,0:T(8,128)(2,1)S(1)} %get-tuple-element.74), channel_id=1, source_target_pairs={{0,96},{32,0},{64,32},{96,64},{1,97},{33,1},{65,33},{97,65},{2,98}... | collective-permute-start | bytes 2211848 | tf_op jit(solution)/shard_map/ppermute | solution.py:432
  98.1 7.4 %term_y.1 = (bf16[288,1024]{1,0:T(8,128)(2,1)S(1)}, bf16[288,1024]{1,0:T(8,128)(2,1)S(1)}, bf16[288,1024]{1,0:T(8,128)(2,1)S(1)}, bf16[288,1024]{1,0:T(8,128)(2,1)S(1)}, f32[8,128]{1,0:T(8,128)S(1)}) custom-call(s32[11]{0:T(128)S(1)} %stack.47.place_ref.after_ref, bf16[8,144,1024]{2,1,0:T(8,128)(2,1)S(1)} %get-tuple-element.53.mine_ref, ...), custom_call_target="tpu_custom_call" | custom-call | flops 1 | bytes 1 | tf_op jit(solution)/shard_map/term_y/pallas_call | solution.py:250
  110.8 17.9 %grads.2 = (bf16[1024,2304]{1,0:T(8,128)(2,1)}, bf16[1024,2304]{1,0:T(8,128)(2,1)}, f32[8,128]{1,0:T(8,128)S(1)}) custom-call(s32[11]{0:T(128)S(1)} %stack.47.place_ref.after_ref, bf16[1024,2304]{1,0:T(8,128)(2,1)} %copy-done.4, bf16[1152,2304]{1,0:T(8,128)(2,1)} %all-gather.3.cloned.1.call-done.same_ref, ...), custom_call_target="tpu_custom_call" | custom-call | flops 1 | bytes 1 | tf_op jit(solution)/shard_map/grads/pallas_call | solution.py:321
  129.3 2.7 %add.79 = (f32[144,1280]{1,0:T(8,128)}, bf16[144,1280]{1,0:T(8,128)(2,1)}) custom-call(bf16[288,1280]{1,0:T(8,128)(2,1)} %copy-done.7, bf16[288,1280]{1,0:T(8,128)(2,1)} %collective-permute-done.17.refs_1_, bf16[288,1280]{1,0:T(8,128)(2,1)} %collective-permute-done.18.refs_2_, bf16[288,1280]{1,0:T(8,128)(2,1)} %collective-permute-done.19.refs_3_, ...), custom_call_target="tpu_custom_call" | custom-call | flops 1 | bytes 1 | tf_op jit(solution)/shard_map/add/pallas_call | solution.py:285
  134.2 2.5 %add.78 = (f32[144,1024]{1,0:T(8,128)}, bf16[144,1024]{1,0:T(8,128)(2,1)}, bf16[144,1024]{1,0:T(8,128)(2,1)}, bf16[144,1024]{1,0:T(8,128)(2,1)}) custom-call(bf16[288,1024]{1,0:T(8,128)(2,1)} %copy-done.10, bf16[288,1024]{1,0:T(8,128)(2,1)} %copy-done.11, bf16[288,1024]{1,0:T(8,128)(2,1)} %collective-permute-done.15.second_low, ...), custom_call_target="tpu_custom_call" | custom-call | flops 1 | bytes 1 | tf_op jit(solution)/shard_map/add/pallas_call | solution.py:285
  139.8 8.2 %grads.3 = (bf16[1024,2304]{1,0:T(8,128)(2,1)}, bf16[1024,2304]{1,0:T(8,128)(2,1)}, f32[8,128]{1,0:T(8,128)S(1)}) custom-call(s32[11]{0:T(128)S(1)} %stack.47.place_ref.after_ref, bf16[1024,2304]{1,0:T(8,128)(2,1)} %copy-done.4, bf16[1152,2304]{1,0:T(8,128)(2,1)} %all-gather.3.cloned.1.call-done.same_ref, ...), custom_call_target="tpu_custom_call", output_to_operand_aliasing={{0}: (7, {}), {1}: (8, {})} | custom-call | flops 1 | bytes 1 | tf_op jit(solution)/shard_map/grads/pallas_call | solution.py:321
  (82 shorter events, 26.7 us)
Async XLA Ops:
  7.2 103.6 %all-gather.3.cloned.1.call-start = ((), (), s32[]{:S(2)}) async-start(), calls=%async_computation | async-start | bytes 5971968 | tf_op jit(solution)/shard_map/all_gather | solution.py:394
  7.9 102.9 %all-gather.5.cloned.1.call-start = ((), (), s32[]{:S(2)}) async-start(), calls=%async_computation.1 | async-start | bytes 5971968 | tf_op jit(solution)/shard_map/all_gather | solution.py:394
  7.9 36.0 %collective-permute-start.4 = (bf16[144,2304]{1,0:T(8,128)(2,1)}, bf16[144,2304]{1,0:T(8,128)(2,1)}, u32[]{:S(2)}, u32[]{:S(2)}) collective-permute-start(bf16[144,2304]{1,0:T(8,128)(2,1)} %bitcast.25), channel_id=1, source_target_pairs={{0,16},{16,0},{1,17},{17,1},{2,18},{18,2},{3,19},{19,3},{4,20},{20... | collective-permute-start | bytes 1990664 | tf_op jit(solution)/shard_map/ppermute | solution.py:381
  11.3 29.3 %collective-permute-start.2 = (bf16[128,2304]{1,0:T(8,128)(2,1)}, bf16[128,2304]{1,0:T(8,128)(2,1)S(1)}, u32[]{:S(2)}, u32[]{:S(2)}) collective-permute-start(bf16[128,2304]{1,0:T(8,128)(2,1)} %refs_0_.1), channel_id=1, source_target_pairs={{0,3},{1,0},{2,1},{3,2},{4,7},{5,4},{6,5},{7,6},{8,11},{9,8},{10,9... | collective-permute-start | bytes 1769480 | tf_op jit(solution)/shard_map/ppermute | solution.py:386
  15.3 28.6 %collective-permute-start.1 = (bf16[128,2304]{1,0:T(8,128)(2,1)}, bf16[128,2304]{1,0:T(8,128)(2,1)S(1)}, u32[]{:S(2)}, u32[]{:S(2)}) collective-permute-start(bf16[128,2304]{1,0:T(8,128)(2,1)} %refs_0_.1), channel_id=1, source_target_pairs={{0,1},{1,2},{2,3},{3,0},{4,5},{5,6},{6,7},{7,4},{8,9},{9,10},{10,1... | collective-permute-start | bytes 1769480 | tf_op jit(solution)/shard_map/ppermute | solution.py:385
  15.3 28.6 %collective-permute-start = (bf16[128,2304]{1,0:T(8,128)(2,1)}, bf16[128,2304]{1,0:T(8,128)(2,1)S(1)}, u32[]{:S(2)}, u32[]{:S(2)}) collective-permute-start(bf16[128,2304]{1,0:T(8,128)(2,1)} %refs_0_.1), channel_id=1, source_target_pairs={{0,4},{4,0},{1,5},{5,1},{2,6},{6,2},{3,7},{7,3},{8,12},{12,8},{9,1... | collective-permute-start | bytes 1769480 | tf_op jit(solution)/shard_map/ppermute | solution.py:384
  16.0 27.9 %collective-permute-start.3 = (bf16[128,2304]{1,0:T(8,128)(2,1)}, bf16[128,2304]{1,0:T(8,128)(2,1)S(1)}, u32[]{:S(2)}, u32[]{:S(2)}) collective-permute-start(bf16[128,2304]{1,0:T(8,128)(2,1)} %refs_0_.1), channel_id=1, source_target_pairs={{0,2},{1,3},{2,0},{3,1},{4,6},{5,7},{6,4},{7,5},{8,10},{9,11},{10,... | collective-permute-start | bytes 1769480 | tf_op jit(solution)/shard_map/ppermute | solution.py:387
  43.9 38.9 %collective-permute-start.11 = (bf16[1024,2304]{1,0:T(8,128)(2,1)}, bf16[1024,2304]{1,0:T(8,128)(2,1)}, u32[]{:S(2)}, u32[]{:S(2)}) collective-permute-start(bf16[1024,2304]{1,0:T(8,128)(2,1)} %copy-done), channel_id=1, source_target_pairs={{0,8},{8,0},{1,9},{9,1},{2,10},{10,2},{3,11},{11,3},{4,12},{12,4},... | collective-permute-start | bytes 14155784 | tf_op jit(solution)/shard_map/ppermute | solution.py:400
  44.0 15.8 %collective-permute-start.7 = (bf16[128,2304]{1,0:T(8,128)(2,1)S(1)}, bf16[128,2304]{1,0:T(8,128)(2,1)}, u32[]{:S(2)}, u32[]{:S(2)}) collective-permute-start(bf16[128,2304]{1,0:T(8,128)(2,1)S(1)} %collective-permute-done.3.refs_3_), channel_id=1, source_target_pairs={{0,4},{4,0},{1,5},{5,1},{2,6},{6,2},{3,7},{7,3},{8,12},{12,8},{9,1... | collective-permute-start | bytes 1769480 | tf_op jit(solution)/shard_map/ppermute | solution.py:398
  44.8 15.5 %collective-permute-start.6 = (bf16[128,2304]{1,0:T(8,128)(2,1)S(1)}, bf16[128,2304]{1,0:T(8,128)(2,1)}, u32[]{:S(2)}, u32[]{:S(2)}) collective-permute-start(bf16[128,2304]{1,0:T(8,128)(2,1)S(1)} %collective-permute-done.refs_4_), channel_id=1, source_target_pairs={{0,3},{1,0},{2,1},{3,2},{4,7},{5,4},{6,5},{7,6},{8,11},{9,8},{10,9... | collective-permute-start | bytes 1769480 | tf_op jit(solution)/shard_map/ppermute | solution.py:397
  45.1 16.4 %collective-permute-start.5 = (bf16[128,2304]{1,0:T(8,128)(2,1)S(1)}, bf16[128,2304]{1,0:T(8,128)(2,1)}, u32[]{:S(2)}, u32[]{:S(2)}) collective-permute-start(bf16[128,2304]{1,0:T(8,128)(2,1)S(1)} %collective-permute-done.refs_4_), channel_id=1, source_target_pairs={{0,1},{1,2},{2,3},{3,0},{4,5},{5,6},{6,7},{7,4},{8,9},{9,10},{10,1... | collective-permute-start | bytes 1769480 | tf_op jit(solution)/shard_map/ppermute | solution.py:396
  46.8 6.0 %collective-permute-start.8 = (s32[1,1024]{1,0:T(1,128)S(1)}, s32[1,1024]{1,0:T(1,128)S(1)}, u32[]{:S(2)}, u32[]{:S(2)}) collective-permute-start(s32[1,1024]{1,0:T(1,128)S(1)} %bitcast.18), channel_id=1, source_target_pairs={{0,8},{8,0},{1,9},{9,1},{2,10},{10,2},{3,11},{11,3},{4,12},{12,4},... | collective-permute-start | bytes 12296 | tf_op jit(solution)/shard_map/ppermute | solution.py:402
  69.9 13.0 %collective-permute-start.10 = (bf16[8,144,1024]{2,1,0:T(8,128)(2,1)S(1)}, bf16[8,144,1024]{2,1,0:T(8,128)(2,1)S(1)}, u32[]{:S(2)}, u32[]{:S(2)}) collective-permute-start(bf16[8,144,1024]{2,1,0:T(8,128)(2,1)S(1)} %get-tuple-element.56), channel_id=1, source_target_pairs={{0,8},{8,0},{1,9},{9,1},{2,10},{10,2},{3,11},{11,3},{4,12},{12,4},... | collective-permute-start | bytes 7077896 | tf_op jit(solution)/shard_map/ppermute | solution.py:419
  70.4 3.7 %collective-permute-start.12 = (f32[32,128]{1,0:T(8,128)S(1)}, f32[32,128]{1,0:T(8,128)S(1)}, u32[]{:S(2)}, u32[]{:S(2)}) collective-permute-start(f32[32,128]{1,0:T(8,128)S(1)} %constant_dynamic-update-slice_fusion), channel_id=1, source_target_pairs={{0,4},{4,0},{1,5},{5,1},{2,6},{6,2},{3,7},{7,3},{8,12},{12,8},{9,1... | collective-permute-start | bytes 49160 | tf_op jit(solution)/shard_map/ppermute | solution.py:421
  77.9 5.0 %collective-permute-start.14 = (f32[32,128]{1,0:T(8,128)S(1)}, f32[32,128]{1,0:T(8,128)S(1)}, u32[]{:S(2)}, u32[]{:S(2)}) collective-permute-start(f32[32,128]{1,0:T(8,128)S(1)} %add.77.squares_ref), channel_id=1, source_target_pairs={{0,3},{3,0},{1,2},{2,1},{4,7},{7,4},{5,6},{6,5},{8,11},{11,8},{9,1... | collective-permute-start | bytes 49160 | tf_op jit(solution)/shard_map/ppermute | solution.py:423
  91.8 37.5 %collective-permute-start.17 = (bf16[288,1280]{1,0:T(8,128)(2,1)S(1)}, bf16[288,1280]{1,0:T(8,128)(2,1)}, u32[]{:S(2)}, u32[]{:S(2)}) collective-permute-start(bf16[288,1280]{1,0:T(8,128)(2,1)S(1)} %get-tuple-element.72), channel_id=1, source_target_pairs={{0,64},{32,96},{64,0},{96,32},{1,65},{33,97},{65,1},{97,33},{2,66}... | collective-permute-start | bytes 2211848 | tf_op jit(solution)/shard_map/ppermute | solution.py:432
  94.9 34.4 %collective-permute-start.18 = (bf16[288,1280]{1,0:T(8,128)(2,1)S(1)}, bf16[288,1280]{1,0:T(8,128)(2,1)}, u32[]{:S(2)}, u32[]{:S(2)}) collective-permute-start(bf16[288,1280]{1,0:T(8,128)(2,1)S(1)} %get-tuple-element.73), channel_id=1, source_target_pairs={{0,32},{32,64},{64,96},{96,0},{1,33},{33,65},{65,97},{97,1},{2,34}... | collective-permute-start | bytes 2211848 | tf_op jit(solution)/shard_map/ppermute | solution.py:432
  95.5 33.8 %collective-permute-start.19 = (bf16[288,1280]{1,0:T(8,128)(2,1)S(1)}, bf16[288,1280]{1,0:T(8,128)(2,1)}, u32[]{:S(2)}, u32[]{:S(2)}) collective-permute-start(bf16[288,1280]{1,0:T(8,128)(2,1)S(1)} %get-tuple-element.74), channel_id=1, source_target_pairs={{0,96},{32,0},{64,32},{96,64},{1,97},{33,1},{65,33},{97,65},{2,98}... | collective-permute-start | bytes 2211848 | tf_op jit(solution)/shard_map/ppermute | solution.py:432
  107.2 26.9 %collective-permute-start.15 = (bf16[288,1024]{1,0:T(8,128)(2,1)S(1)}, bf16[288,1024]{1,0:T(8,128)(2,1)}, u32[]{:S(2)}, u32[]{:S(2)}) collective-permute-start(bf16[288,1024]{1,0:T(8,128)(2,1)S(1)} %get-tuple-element.62), channel_id=1, source_target_pairs={{0,16},{16,0},{1,17},{17,1},{2,18},{18,2},{3,19},{19,3},{4,20},{20... | collective-permute-start | bytes 1769480 | tf_op jit(solution)/shard_map/ppermute | solution.py:434
  109.4 24.8 %collective-permute-start.16 = (bf16[288,1024]{1,0:T(8,128)(2,1)S(1)}, bf16[288,1024]{1,0:T(8,128)(2,1)}, u32[]{:S(2)}, u32[]{:S(2)}) collective-permute-start(bf16[288,1024]{1,0:T(8,128)(2,1)S(1)} %get-tuple-element.63), channel_id=1, source_target_pairs={{0,16},{16,0},{1,17},{17,1},{2,18},{18,2},{3,19},{19,3},{4,20},{20... | collective-permute-start | bytes 1769480 | tf_op jit(solution)/shard_map/ppermute | solution.py:434
  132.0 17.8 %collective-permute-start.20 = (bf16[144,1280]{1,0:T(8,128)(2,1)}, bf16[144,1280]{1,0:T(8,128)(2,1)S(1)}, u32[]{:S(2)}, u32[]{:S(2)}) collective-permute-start(bf16[144,1280]{1,0:T(8,128)(2,1)} %get-tuple-element.76), channel_id=1, source_target_pairs={{0,16},{16,0},{1,17},{17,1},{2,18},{18,2},{3,19},{19,3},{4,20},{20... | collective-permute-start | bytes 1105928 | tf_op jit(solution)/shard_map/ppermute | solution.py:443
  136.7 11.4 %collective-permute-start.21 = (bf16[144,1024]{1,0:T(8,128)(2,1)}, bf16[144,1024]{1,0:T(8,128)(2,1)S(1)}, u32[]{:S(2)}, u32[]{:S(2)}) collective-permute-start(bf16[144,1024]{1,0:T(8,128)(2,1)} %get-tuple-element.78), channel_id=1, source_target_pairs={{0,64},{32,96},{64,0},{96,32},{1,65},{33,97},{65,1},{97,33},{2,66}... | collective-permute-start | bytes 884744 | tf_op jit(solution)/shard_map/ppermute | solution.py:445
  136.7 13.1 %collective-permute-start.23 = (bf16[144,1024]{1,0:T(8,128)(2,1)}, bf16[144,1024]{1,0:T(8,128)(2,1)S(1)}, u32[]{:S(2)}, u32[]{:S(2)}) collective-permute-start(bf16[144,1024]{1,0:T(8,128)(2,1)} %get-tuple-element.79), channel_id=1, source_target_pairs={{0,96},{32,0},{64,32},{96,64},{1,97},{33,1},{65,33},{97,65},{2,98}... | collective-permute-start | bytes 884744 | tf_op jit(solution)/shard_map/ppermute | solution.py:445
  138.8 11.0 %collective-permute-start.22 = (bf16[144,1024]{1,0:T(8,128)(2,1)}, bf16[144,1024]{1,0:T(8,128)(2,1)S(1)}, u32[]{:S(2)}, u32[]{:S(2)}) collective-permute-start(bf16[144,1024]{1,0:T(8,128)(2,1)} %get-tuple-element.66.refs_0_), channel_id=1, source_target_pairs={{0,32},{32,64},{64,96},{96,0},{1,33},{33,65},{65,97},{97,1},{2,34}... | collective-permute-start | bytes 884744 | tf_op jit(solution)/shard_map/ppermute | solution.py:445
  (19 other events, 222.7 us)
Sparse Core Ops, SparseCore 0:
  9.7 42.8 all-gather.2
  54.2 33.8 all-gather.4

commit v3 on v2

--- a/solution.py
+++ b/solution.py
@@ -60,15 +60,10 @@
         in_specs=[spec, spec],
         out_specs=spec,
         out_shape=jax.ShapeDtypeStruct(gate.shape, jnp.bfloat16),
-        compiler_params=params(40, "arbitrary"),
+        compiler_params=params(16, "arbitrary"),
         cost_estimate=LITTLE,
         name="hidden",
     )(gate, up)
-
-
-def tiles_of(rows):
-    count = rows // TILE
-    return [(i, j) for i in range(count) for j in range(i, count)]
 
 
 def outer(left, right):
@@ -77,80 +72,115 @@
     )
 
 
-def hidden_gram_kernel(hidden_ref, user_ref, user_row_ref, gram_ref):
-    for k, (i, j) in enumerate(tiles_of(hidden_ref.shape[0])):
-        first, second = pl.ds(i * TILE, TILE), pl.ds(j * TILE, TILE)
-        tile = outer(hidden_ref[first, :], hidden_ref[second, :])
-        same = user_ref[first, :] == user_row_ref[:, second]
-        gram_ref[k] = jnp.where(same, tile if i == j else 2.0 * tile, 0.0)
-
-
-def hidden_gram_call(hidden, user, user_row):
+def starts_of(place_ref, size):
+    return [pl.multiple_of(place_ref[3 + k], size) for k in range(NP * NZ)]
+
+
+def hidden_gram_kernel(
+    place_ref, hidden_ref, user_ref, user_row_ref, ee_ref, la_ref, row_ref, rows, users
+):
+    size = rows.shape[0] // (NP * NZ)
+    early = ee_ref.shape[0]
+    for k, start in enumerate(starts_of(place_ref, size)):
+        inside = pl.ds(k * size, size)
+        rows[inside, :] = hidden_ref[pl.ds(start, size), :]
+        users[inside, :] = user_ref[pl.ds(start, size), :]
+        row_ref[:, inside] = user_row_ref[:, pl.ds(start, size)]
+    gram = outer(rows[:early, :], rows[:early, :])
+    ee_ref[...] = jnp.where(users[:early, :] == row_ref[:, :early], gram, 0.0)
+    for columns, weight in ((slice(0, early), 2.0), (slice(early, rows.shape[0]), 1.0)):
+        gram = weight * outer(rows[early:, :], rows[columns, :])
+        la_ref[:, columns] = jnp.where(users[early:, :] == row_ref[:, columns], gram, 0.0)
+
+
+def hidden_gram_call(place, hidden, user, user_row, early):
     rows, cols = hidden.shape
-    count = len(tiles_of(rows))
+    late = rows - early
+    gram = lambda a, b: jax.ShapeDtypeStruct((a, b), jnp.float32)
     return pl.pallas_call(
         hidden_gram_kernel,
-        in_specs=[VMEM, VMEM, VMEM],
-        out_specs=VMEM,
-        out_shape=jax.ShapeDtypeStruct((count, TILE, TILE), jnp.float32),
-        compiler_params=params(24),
+        in_specs=[SMEM, VMEM, VMEM, VMEM],
+        out_specs=[VMEM] * 3,
+        out_shape=[
+            gram(early, early),
+            gram(late, rows),
+            jax.ShapeDtypeStruct((1, rows), jnp.int32),
+        ],
+        scratch_shapes=[pltpu.VMEM((rows, cols), jnp.bfloat16), pltpu.VMEM((rows, 1), jnp.int32)],
+        compiler_params=params(20),
         cost_estimate=LITTLE,
         name="hidden_gram",
-    )(hidden, user, user_row)
-
-
-def grad_gram_kernel(place_ref, *refs):
-    count = len(refs) - 5
-    pieces = refs[:count]
-    gram_ref, user_row_ref, grad_ref, squares_ref, sems = refs[count:]
-    copies = []
-    for k, piece in enumerate(pieces):
-        size = piece.shape[0]
-        start = pl.multiple_of(place_ref[k + 3], size)
-        copies.append(pltpu.make_async_copy(piece, grad_ref.at[pl.ds(start, size)], sems.at[k]))
+    )(place, hidden, user, user_row)
+
+
+def gather_blocks(pieces, out_ref, first, sems):
+    size = pieces[0].shape[0]
+    copies = [
+        pltpu.make_async_copy(piece, out_ref.at[pl.ds((first + k) * size, size)], sems.at[k])
+        for k, piece in enumerate(pieces)
+    ]
     for copy in copies:
         copy.start()
     for copy in copies:
         copy.wait()
-    rows = grad_ref.shape[0]
-    terms = [None] * (rows // TILE)
-    for k, (i, j) in enumerate(tiles_of(rows)):
-        tile = outer(grad_ref[pl.ds(i * TILE, TILE), :], grad_ref[pl.ds(j * TILE, TILE), :])
-        term = jnp.sum(tile * gram_ref[k], axis=0, keepdims=True)
-        terms[j] = term if terms[j] is None else terms[j] + term
-    terms = jnp.concatenate(terms, axis=1)
-    users = lax.broadcasted_iota(jnp.int32, (squares_ref.shape[0], rows), 0)
-    chosen = jnp.where(users == user_row_ref[...], terms, 0.0)
-    squares_ref[...] = jnp.broadcast_to(
-        jnp.sum(chosen, axis=1, keepdims=True), squares_ref.shape
-    )
-
-
-def grad_gram_call(place, pieces, gram, user_row, users_group):
-    rows, cols = user_row.shape[1], pieces[0].shape[1]
-    return pl.pallas_call(
-        grad_gram_kernel,
-        in_specs=[SMEM] + [ANY] * len(pieces) + [VMEM] * 2,
+
+
+def by_user(terms, row, count):
+    users = lax.broadcasted_iota(jnp.int32, (count, terms.shape[1]), 0)
+    return jnp.sum(jnp.where(users == row, terms, 0.0), axis=1, keepdims=True)
+
+
+def early_gram_kernel(*refs):
+    pieces, (gram_ref, row_ref, out_ref, squares_ref, sems) = refs[:-5], refs[-5:]
+    gather_blocks(pieces, out_ref, 0, sems)
+    early = gram_ref.shape[0]
+    gram = outer(out_ref[:early, :], out_ref[:early, :]) * gram_ref[...]
+    terms = jnp.sum(gram, axis=0, keepdims=True)
+    squares = by_user(terms, row_ref[:, :early], squares_ref.shape[0])
+    squares_ref[...] = jnp.broadcast_to(squares, squares_ref.shape)
+
+
+def late_gram_kernel(*refs):
+    pieces, (gram_ref, row_ref, first_ref, _, out_ref, squares_ref, sems) = refs[:-7], refs[-7:]
+    late, rows = gram_ref.shape
+    gather_blocks(pieces, out_ref, NP * NZ - len(pieces), sems)
+    gram = outer(out_ref[rows - late :, :], out_ref[...]) * gram_ref[...]
+    terms = jnp.sum(gram, axis=0, keepdims=True)
+    squares_ref[...] = first_ref[...] + by_user(terms, row_ref[...], squares_ref.shape[0])
+
+
+def gram_call(kernel, pieces, others, users_group, name, held=()):
+    size, cols = pieces[0].shape
+    inputs = [*pieces, *others, *held]
+    return pl.pallas_call(
+        kernel,
+        in_specs=[ANY] * len(pieces) + [VMEM] * (len(inputs) - len(pieces)),
         out_specs=[VMEM] * 2,
         out_shape=[
-            jax.ShapeDtypeStruct((rows, cols), jnp.bfloat16),
+            jax.ShapeDtypeStruct((NP * NZ * size, cols), jnp.bfloat16),
             jax.ShapeDtypeStruct((users_group, 128), jnp.float32),
         ],
         scratch_shapes=[pltpu.SemaphoreType.DMA((len(pieces),))],
-        compiler_params=params(40),
-        cost_estimate=LITTLE,
-        name="grad_gram",
-    )(place, *pieces, gram, user_row)
+        input_output_aliases={len(inputs) - 1: 0} if held else {},
+        compiler_params=params(20),
+        cost_estimate=LITTLE,
+        name=name,
+    )(*inputs)
 
 
 def transpose_kernel(place_ref, grad_ref, mine_ref, other_ref):
     core = place_ref[0]
-    count, width, _ = mine_ref.shape
-    turned = grad_ref[...].T
-    for k in range(count):
-        first, second = (turned[(2 * k + i) * width : (2 * k + i + 1) * width] for i in range(2))
-        mine_ref[k] = jnp.where(core == 0, first, second)
-        other_ref[k] = jnp.where(core == 0, second, first)
+    count, width, rows = mine_ref.shape
+    size = rows // (NP * NZ)
+    for n, start in enumerate(starts_of(place_ref, size)):
+        turned = grad_ref[pl.ds(n * size, size), :].T
+        inside = pl.ds(start, size)
+        for k in range(count):
+            first, second = (
+                turned[(2 * k + i) * width : (2 * k + i + 1) * width] for i in range(2)
+            )
+            mine_ref[k, :, inside] = jnp.where(core == 0, first, second)
+            other_ref[k, :, inside] = jnp.where(core == 0, second, first)
 
 
 def transpose_call(place, grad, width):
@@ -295,8 +325,15 @@
     )(*parts, *extra)
 
 
-def grads_kernel(place_ref, grad_ref, same_ref, other_ref, gate_ref, up_ref, *refs):
-    gate_grad_ref, up_grad_ref, token_ref, weight_ref = refs[-4:]
+def grads_kernel(place_ref, blocks_ref, same_ref, other_ref, gate_ref, up_ref, *refs):
+    gate_grad_ref, up_grad_ref, token_ref, grad_ref, weight_ref = refs[-5:]
+
+    @pl.when(pl.program_id(0) == 0)
+    def _():
+        size = grad_ref.shape[0] // (NP * NZ)
+        for k, start in enumerate(starts_of(place_ref, size)):
+            grad_ref[pl.ds(start, size), :] = blocks_ref[pl.ds(k * size, size), :]
+
     width = weight_ref.shape[0] // (NX * NY * NC)
     y_index = place_ref[2]
     for k in range(NX * NC):
@@ -313,9 +350,9 @@
     up_grad_ref[...] = (hidden_grad * gelu_value).astype(jnp.bfloat16)
 
 
-def grads_call(place, grad, weights, gate, up, after, first, steps, held):
-    rows, depth = grad.shape
-    cols = gate.shape[1]
+def grads_call(place, blocks, weights, gate, up, after, first, steps, held):
+    rows, cols = gate.shape
+    depth = blocks.shape[1]
     weight = pl.BlockSpec((depth // 2, TILE), lambda n: (0, n + first))
     tile = pl.BlockSpec((rows, TILE), lambda n: (0, n + first))
     return pl.pallas_call(
@@ -333,12 +370,14 @@
         + [ANY] * len(held),
         out_specs=[tile, tile, pl.BlockSpec(TOKEN.shape, lambda n: (0, 0))],
         out_shape=[jax.ShapeDtypeStruct((rows, cols), jnp.bfloat16)] * 2 + [TOKEN],
-        scratch_shapes=[pltpu.VMEM((depth, TILE), jnp.bfloat16)],
+        scratch_shapes=[
+            pltpu.VMEM((rows, depth), jnp.bfloat16), pltpu.VMEM((depth, TILE), jnp.bfloat16)
+        ],
         input_output_aliases={7 + k: k for k in range(len(held))},
         compiler_params=params(52, "arbitrary"),
         cost_estimate=LITTLE,
         name="grads",
-    )(place, grad, *weights, gate, up, after, *held)
+    )(place, blocks, *weights, gate, up, after, *held)
 
 
 def update_kernel(scale, own_x, got_x, own_y, *refs):
@@ -400,20 +439,31 @@
     hidden_sib = lax.ppermute(hidden, "c", shift(NC, 1))
     user_row = token_user.reshape(1, rows)
     user_sib = lax.ppermute(user_row, "c", shift(NC, 1))
-    gram = hidden_gram_call(hidden, token_user, user_row)
-
-    other_left, other_right, other_far, user_sib, gram = lax.optimization_barrier(
-        (other_left, other_right, other_far, user_sib, gram)
-    )
-    pieces = [out_grad, left, right, far, other, other_left, other_right, other_far]
     place = [
         (at * NZ + (ring + step) % NZ) * out_grad.shape[0]
         for at in (pair, 1 - pair)
         for step in (0, 3, 1, 2)
     ]
     place = jnp.stack([core, x_index, y_index, *place]).astype(jnp.int32)
-    grad_rows, squares = grad_gram_call(place, pieces, gram, user_row, users_group)
-    mine, others = transpose_call(place, grad_rows, width)
+    pieces = [out_grad, left, right, far, other]
+    gram_early, gram_late, user_order = hidden_gram_call(
+        place, hidden, token_user, user_row, len(pieces) * out_grad.shape[0]
+    )
+    blocks, squares = gram_call(
+        early_gram_kernel, pieces, [gram_early, user_order], users_group, "early_gram"
+    )
+    other_left, other_right, other_far, user_sib, squares = lax.optimization_barrier(
+        (other_left, other_right, other_far, user_sib, squares)
+    )
+    blocks, squares = gram_call(
+        late_gram_kernel,
+        [other_left, other_right, other_far],
+        [gram_late, user_order, squares],
+        users_group,
+        "late_gram",
+        (blocks,),
+    )
+    mine, others = transpose_call(place, blocks, width)
     squares_sib = lax.ppermute(squares, "c", shift(NC, 1))
     squares_sib, others = lax.optimization_barrier((squares_sib, others))
     theirs = lax.ppermute(others, "c", shift(NC, 1))
@@ -434,8 +484,8 @@
     got_y = [lax.ppermute(part, "yh", shift(NY, 1)) for part in term_y[2:]]
 
     steps = cols // TILE
-    early = (2 * steps) // 3 + 1
-    *held, done = grads_call(place, grad_rows, weights, gate_pre, up_pre, done, 0, early, ())
+    split_steps = (2 * steps) // 3 + 1
+    *held, done = grads_call(place, blocks, weights, gate_pre, up_pre, done, 0, split_steps, ())
 
     keep_x, send_x = add_call(
         add_x_kernel, [term_x[0], *got_x.values()], width, 1, (done,)
@@ -445,7 +495,7 @@
     last_y = [lax.ppermute(send_y[dx - 1], "x", shift(NX, dx)) for dx in (2, 1, 3)]
 
     gate_grad, up_grad, done = grads_call(
-        place, grad_rows, weights, gate_pre, up_pre, send_y[0], early, steps - early, held
+        place, blocks, weights, gate_pre, up_pre, send_y[0], split_steps, steps - split_steps, held
     )
     scale = math.sqrt(F * D) / (users_group * groups * clip_bound)
     weight_update = update_call(

time: 159 us -> 158 us (level)
  waiting for transfers between devices: 36 us -> 30.2 us
  Pallas kernels: 64.5 us -> 68.3 us
  local copies, waits for them, and re-layouts: 13.2 us -> 15.7 us
    ppermute x1, waiting for transfers between devices: 7.05 us -> 1.01 us  [local(): other_far = lax.ppermute(far, 'yl', shift(NP, 1))]
    pallas_call x2 -> x3, Pallas kernels: 9.21 us -> 11.9 us  [the longest x2 6.56 us: gram_call(): pl.pallas_call(kernel, in_specs=[ANY] * len(pieces) + [VMEM] * (len(input...]
    unnamed x36 -> x46, local copies, waits for them, and re-layouts: 13.1 us -> 15.6 us
  transfers between devices with their start and end apart: 26 -> 26, of which waited for: 9 -> 11; matrix products, arithmetic and copies ran while one was open for 0% -> 0% of each run, Pallas kernels for 40% -> 42%
where the time goes in v3:
time: 158 us; the launch traced here: 157 us
  Pallas kernels  68.3 us (43%)
  waiting for transfers between devices  30.2 us (19%)
  starting transfers between devices  29 us (18%)
  local copies, waits for them, and re-layouts  15.7 us (10%)
  between operations  14.3 us (9%)
    pallas_call x2, Pallas kernels, grads_call(): pl.pallas_call(grads_kernel, grid=(steps,), in_specs=[SMEM, pl.BlockSpec(...  26.8 us
    pallas_call x2, Pallas kernels, term_call(): pl.pallas_call(functools.partial(term_kernel, clip_bound, by_x), grid=(co...  16.8 us
    unnamed x46, local copies, waits for them, and re-layouts  15.6 us
    ppermute x1, waiting for transfers between devices, local(): right = lax.ppermute(out_grad, 'z', shift(NZ, -1))  11.9 us
    pallas_call x2, Pallas kernels, gram_call(): pl.pallas_call(kernel, in_specs=[ANY] * len(pieces) + [VMEM] * (len(input...  6.56 us
    ppermute x3, starting transfers between devices, local(): lax.ppermute(term_x[dx], 'x', shift(NX, dx))  6.34 us
    pallas_call x1, Pallas kernels, hidden_gram_call(): pl.pallas_call(hidden_gram_kernel, in_specs=[SMEM, VMEM, VMEM, VMEM], out...  5.36 us
    pallas_call x2, Pallas kernels, add_call(): pl.pallas_call(kernel, grid=(2,), in_specs=[tile(a.shape[0]) for a in par...  5.24 us
  transfers between devices with their start and end apart: 26, of which 11 were waited for; matrix products, arithmetic and copies ran while one was open for 0% of the time, Pallas kernels for 42%

profile of v3, /device:TPU:0, one launch (start us, length us, event | category | flops | bytes accessed | tf_op | source)
XLA Modules:
  0.0 157.4 jit_solution(118605165245747466)
XLA Ops:
  7.9 3.4 %collective-permute-start.4 = (bf16[144,2304]{1,0:T(8,128)(2,1)}, bf16[144,2304]{1,0:T(8,128)(2,1)S(1)}, u32[]{:S(2)}, u32[]{:S(2)}) collective-permute-start(bf16[144,2304]{1,0:T(8,128)(2,1)} %bitcast.24), channel_id=1, source_target_pairs={{0,16},{16,0},{1,17},{17,1},{2,18},{18,2},{3,19},{19,3},{4,20},{20... | collective-permute-start | bytes 1990664 | tf_op jit(solution)/shard_map/ppermute | solution.py:420
  11.3 4.0 %collective-permute-start.2 = (bf16[128,2304]{1,0:T(8,128)(2,1)}, bf16[128,2304]{1,0:T(8,128)(2,1)S(1)}, u32[]{:S(2)}, u32[]{:S(2)}) collective-permute-start(bf16[128,2304]{1,0:T(8,128)(2,1)} %refs_0_.1), channel_id=1, source_target_pairs={{0,3},{1,0},{2,1},{3,2},{4,7},{5,4},{6,5},{7,6},{8,11},{9,8},{10,9... | collective-permute-start | bytes 1769480 | tf_op jit(solution)/shard_map/ppermute | solution.py:425
  17.9 2.3 %copy-done.3 = bf16[1024,2304]{1,0:T(8,128)(2,1)S(1)} copy-done((bf16[1024,2304]{1,0:T(8,128)(2,1)S(1)}, bf16[1024,2304]{1,0:T(8,128)(2,1)}, u32[]{:S(2)}) %copy-start.3) | copy-done | bytes 4718616
  20.2 2.7 %copy-done.4 = bf16[1024,2304]{1,0:T(8,128)(2,1)S(1)} copy-done((bf16[1024,2304]{1,0:T(8,128)(2,1)S(1)}, bf16[1024,2304]{1,0:T(8,128)(2,1)}, u32[]{:S(2)}) %copy-start.4) | copy-done | bytes 4718616
  22.9 3.6 %hidden.1.hidden_ref.own_ref = bf16[1024,2304]{1,0:T(8,128)(2,1)S(1)} custom-call(bf16[1024,2304]{1,0:T(8,128)(2,1)S(1)} %copy-done.3, bf16[1024,2304]{1,0:T(8,128)(2,1)S(1)} %copy-done.4), custom_call_target="tpu_custom_call" | custom-call | flops 1 | bytes 1 | tf_op jit(solution)/shard_map/hidden/pallas_call | solution.py:57
  26.6 2.2 %copy-done = bf16[1024,2304]{1,0:T(8,128)(2,1)} copy-done((bf16[1024,2304]{1,0:T(8,128)(2,1)}, bf16[1024,2304]{1,0:T(8,128)(2,1)S(1)}, u32[]{:S(2)}) %copy-start) | copy-done | bytes 4718616
  28.8 11.9 %collective-permute-done.2.refs_2_ = bf16[128,2304]{1,0:T(8,128)(2,1)S(1)} collective-permute-done((bf16[128,2304]{1,0:T(8,128)(2,1)}, bf16[128,2304]{1,0:T(8,128)(2,1)S(1)}, u32[]{:S(2)}, u32[]{:S(2)}) %collective-permute-start.2) | collective-permute-done | bytes 589856 | tf_op jit(solution)/shard_map/ppermute | solution.py:425
  41.4 2.5 %collective-permute-done.1.refs_1_ = bf16[128,2304]{1,0:T(8,128)(2,1)S(1)} collective-permute-done((bf16[128,2304]{1,0:T(8,128)(2,1)}, bf16[128,2304]{1,0:T(8,128)(2,1)S(1)}, u32[]{:S(2)}, u32[]{:S(2)}) %collective-permute-start.1) | collective-permute-done | bytes 589856 | tf_op jit(solution)/shard_map/ppermute | solution.py:424
  48.8 2.3 %copy-done.1 = bf16[1024,2304]{1,0:T(8,128)(2,1)S(1)} copy-done((bf16[1024,2304]{1,0:T(8,128)(2,1)S(1)}, bf16[1024,2304]{1,0:T(8,128)(2,1)}, u32[]{:S(2)}) %copy-start.1) | copy-done | bytes 4718616
  51.2 5.4 %hidden_gram.1 = (f32[640,640]{1,0:T(8,128)S(1)}, f32[384,1024]{1,0:T(8,128)S(1)}, s32[1,1024]{1,0:T(1,128)S(1)}) custom-call(s32[11]{0:T(128)S(1)} %stack.47.place_ref.after_ref, bf16[1024,2304]{1,0:T(8,128)(2,1)S(1)} %copy-done.1, s32[1024,1]{1,0:T(8,128)S(1)} %copy.12.user_ref, s32[1,1024]{1,0:T(1,128)S(1)} %bitcast.19), custom_call_target="tpu_custom_call" | custom-call | flops 1 | bytes 1 | tf_op jit(solution)/shard_map/hidden_gram/pallas_call | solution.py:100
  56.6 4.0 %early_gram.1 = (bf16[1024,2304]{1,0:T(8,128)(2,1)S(1)}, f32[16,128]{1,0:T(8,128)S(1)}) custom-call(bf16[128,2304]{1,0:T(8,128)(2,1)S(1)} %copy-done.9, bf16[128,2304]{1,0:T(8,128)(2,1)S(1)} %copy-done.13, bf16[128,2304]{1,0:T(8,128)(2,1)S(1)} %copy-done.11, bf16[128,2304]{1,0:T(8,128)(2,1)} %collective-permute-done.3.refs_3_, ...), custom_call_target="tpu_custom_call" | custom-call | flops 1 | bytes 1 | tf_op jit(solution)/shard_map/early_gram/pallas_call | solution.py:155
  63.9 2.5 %late_gram.1 = (bf16[1024,2304]{1,0:T(8,128)(2,1)S(1)}, f32[16,128]{1,0:T(8,128)S(1)}) custom-call(bf16[128,2304]{1,0:T(8,128)(2,1)S(1)} %collective-permute-done.5.refs_0_, bf16[128,2304]{1,0:T(8,128)(2,1)S(1)} %collective-permute-done.6.refs_1_, bf16[128,2304]{1,0:T(8,128)(2,1)S(1)} %collective-permute-done.7.refs_2_, ...), custom_call_target="tpu_custom_call", output_to_operand_aliasing={{0}: (6, {})} | custom-call | flops 1 | bytes 1 | tf_op jit(solution)/shard_map/late_gram/pallas_call | solution.py:155
  66.5 2.1 %transpose.17 = (bf16[8,144,1024]{2,1,0:T(8,128)(2,1)S(1)}, bf16[8,144,1024]{2,1,0:T(8,128)(2,1)S(1)}) custom-call(s32[11]{0:T(128)S(1)} %stack.47.place_ref.after_ref, bf16[1024,2304]{1,0:T(8,128)(2,1)S(1)} %get-tuple-element.61.grad_ref.blocks_ref), custom_call_target="tpu_custom_call" | custom-call | flops 1 | bytes 1 | tf_op jit(solution)/shard_map/transpose/pallas_call | solution.py:190
  70.5 2.4 %collective-permute-done.12 = f32[32,128]{1,0:T(8,128)S(1)} collective-permute-done((f32[32,128]{1,0:T(8,128)S(1)}, f32[32,128]{1,0:T(8,128)S(1)}, u32[]{:S(2)}, u32[]{:S(2)}) %collective-permute-start.12) | collective-permute-done | bytes 16416 | tf_op jit(solution)/shard_map/ppermute | solution.py:471
  72.9 3.7 %collective-permute-done.13 = f32[32,128]{1,0:T(8,128)S(1)} collective-permute-done((f32[32,128]{1,0:T(8,128)S(1)}, f32[32,128]{1,0:T(8,128)S(1)}, u32[]{:S(2)}, u32[]{:S(2)}) %collective-permute-start.13) | collective-permute-done | bytes 16416 | tf_op jit(solution)/shard_map/ppermute | solution.py:472
  77.0 4.7 %collective-permute-done.14.more_ref = f32[32,128]{1,0:T(8,128)S(1)} collective-permute-done((f32[32,128]{1,0:T(8,128)S(1)}, f32[32,128]{1,0:T(8,128)S(1)}, u32[]{:S(2)}, u32[]{:S(2)}) %collective-permute-start.14) | collective-permute-done | bytes 16416 | tf_op jit(solution)/shard_map/ppermute | solution.py:473
  81.7 8.9 %term_x.1 = (bf16[288,1280]{1,0:T(8,128)(2,1)S(1)}, bf16[288,1280]{1,0:T(8,128)(2,1)S(1)}, bf16[288,1280]{1,0:T(8,128)(2,1)S(1)}, bf16[288,1280]{1,0:T(8,128)(2,1)S(1)}, f32[8,128]{1,0:T(8,128)S(1)}) custom-call(s32[11]{0:T(128)S(1)} %stack.47.place_ref.after_ref, bf16[8,144,1024]{2,1,0:T(8,128)(2,1)S(1)} %get-tuple-element.63.mine_ref, ...), custom_call_target="tpu_custom_call" | custom-call | flops 1 | bytes 1 | tf_op jit(solution)/shard_map/term_x/pallas_call | solution.py:280
  90.5 3.1 %collective-permute-start.17 = (bf16[288,1280]{1,0:T(8,128)(2,1)S(1)}, bf16[288,1280]{1,0:T(8,128)(2,1)}, u32[]{:S(2)}, u32[]{:S(2)}) collective-permute-start(bf16[288,1280]{1,0:T(8,128)(2,1)S(1)} %get-tuple-element.82), channel_id=1, source_target_pairs={{0,64},{32,96},{64,0},{96,32},{1,65},{33,97},{65,1},{97,33},{2,66}... | collective-permute-start | bytes 2211848 | tf_op jit(solution)/shard_map/ppermute | solution.py:482
  94.2 2.6 %collective-permute-start.19 = (bf16[288,1280]{1,0:T(8,128)(2,1)S(1)}, bf16[288,1280]{1,0:T(8,128)(2,1)}, u32[]{:S(2)}, u32[]{:S(2)}) collective-permute-start(bf16[288,1280]{1,0:T(8,128)(2,1)S(1)} %get-tuple-element.84), channel_id=1, source_target_pairs={{0,96},{32,0},{64,32},{96,64},{1,97},{33,1},{65,33},{97,65},{2,98}... | collective-permute-start | bytes 2211848 | tf_op jit(solution)/shard_map/ppermute | solution.py:482
  96.9 8.0 %term_y.1 = (bf16[288,1024]{1,0:T(8,128)(2,1)S(1)}, bf16[288,1024]{1,0:T(8,128)(2,1)S(1)}, bf16[288,1024]{1,0:T(8,128)(2,1)}, bf16[288,1024]{1,0:T(8,128)(2,1)S(1)}, f32[8,128]{1,0:T(8,128)S(1)}) custom-call(s32[11]{0:T(128)S(1)} %stack.47.place_ref.after_ref, bf16[8,144,1024]{2,1,0:T(8,128)(2,1)S(1)} %get-tuple-element.63.mine_ref, ...), custom_call_target="tpu_custom_call" | custom-call | flops 1 | bytes 1 | tf_op jit(solution)/shard_map/term_y/pallas_call | solution.py:280
  110.1 18.2 %grads.2 = (bf16[1024,2304]{1,0:T(8,128)(2,1)}, bf16[1024,2304]{1,0:T(8,128)(2,1)}, f32[8,128]{1,0:T(8,128)S(1)}) custom-call(s32[11]{0:T(128)S(1)} %stack.47.place_ref.after_ref, bf16[1024,2304]{1,0:T(8,128)(2,1)} %copy-done.2, bf16[1152,2304]{1,0:T(8,128)(2,1)} %all-gather.3.cloned.1.call-done.same_ref, ...), custom_call_target="tpu_custom_call" | custom-call | flops 1 | bytes 1 | tf_op jit(solution)/shard_map/grads/pallas_call | solution.py:358
  129.0 2.7 %add.79 = (f32[144,1280]{1,0:T(8,128)}, bf16[144,1280]{1,0:T(8,128)(2,1)}) custom-call(bf16[288,1280]{1,0:T(8,128)(2,1)} %copy-done.7, bf16[288,1280]{1,0:T(8,128)(2,1)} %collective-permute-done.17.refs_1_, bf16[288,1280]{1,0:T(8,128)(2,1)} %collective-permute-done.18.refs_2_, bf16[288,1280]{1,0:T(8,128)(2,1)} %collective-permute-done.19.refs_3_, ...), custom_call_target="tpu_custom_call" | custom-call | flops 1 | bytes 1 | tf_op jit(solution)/shard_map/add/pallas_call | solution.py:315
  133.6 2.5 %add.78 = (f32[144,1024]{1,0:T(8,128)}, bf16[144,1024]{1,0:T(8,128)(2,1)}, bf16[144,1024]{1,0:T(8,128)(2,1)}, bf16[144,1024]{1,0:T(8,128)(2,1)}) custom-call(bf16[288,1024]{1,0:T(8,128)(2,1)} %copy-done.14, bf16[288,1024]{1,0:T(8,128)(2,1)} %copy-done.15, bf16[288,1024]{1,0:T(8,128)(2,1)} %collective-permute-done.15.second_low, ...), custom_call_target="tpu_custom_call" | custom-call | flops 1 | bytes 1 | tf_op jit(solution)/shard_map/add/pallas_call | solution.py:315
  139.3 8.5 %grads.3 = (bf16[1024,2304]{1,0:T(8,128)(2,1)}, bf16[1024,2304]{1,0:T(8,128)(2,1)}, f32[8,128]{1,0:T(8,128)S(1)}) custom-call(s32[11]{0:T(128)S(1)} %stack.47.place_ref.after_ref, bf16[1024,2304]{1,0:T(8,128)(2,1)} %copy-done.2, bf16[1152,2304]{1,0:T(8,128)(2,1)} %all-gather.3.cloned.1.call-done.same_ref, ...), custom_call_target="tpu_custom_call", output_to_operand_aliasing={{0}: (7, {}), {1}: (8, {})} | custom-call | flops 1 | bytes 1 | tf_op jit(solution)/shard_map/grads/pallas_call | solution.py:358
  (93 shorter events, 28.8 us)
Async XLA Ops:
  7.2 103.0 %all-gather.3.cloned.1.call-start = ((), (), s32[]{:S(2)}) async-start(), calls=%async_computation | async-start | bytes 5971968 | tf_op jit(solution)/shard_map/all_gather | solution.py:433
  7.9 102.2 %all-gather.5.cloned.1.call-start = ((), (), s32[]{:S(2)}) async-start(), calls=%async_computation.1 | async-start | bytes 5971968 | tf_op jit(solution)/shard_map/all_gather | solution.py:433
  7.9 36.8 %collective-permute-start.4 = (bf16[144,2304]{1,0:T(8,128)(2,1)}, bf16[144,2304]{1,0:T(8,128)(2,1)S(1)}, u32[]{:S(2)}, u32[]{:S(2)}) collective-permute-start(bf16[144,2304]{1,0:T(8,128)(2,1)} %bitcast.24), channel_id=1, source_target_pairs={{0,16},{16,0},{1,17},{17,1},{2,18},{18,2},{3,19},{19,3},{4,20},{20... | collective-permute-start | bytes 1990664 | tf_op jit(solution)/shard_map/ppermute | solution.py:420
  11.3 29.3 %collective-permute-start.2 = (bf16[128,2304]{1,0:T(8,128)(2,1)}, bf16[128,2304]{1,0:T(8,128)(2,1)S(1)}, u32[]{:S(2)}, u32[]{:S(2)}) collective-permute-start(bf16[128,2304]{1,0:T(8,128)(2,1)} %refs_0_.1), channel_id=1, source_target_pairs={{0,3},{1,0},{2,1},{3,2},{4,7},{5,4},{6,5},{7,6},{8,11},{9,8},{10,9... | collective-permute-start | bytes 1769480 | tf_op jit(solution)/shard_map/ppermute | solution.py:425
  15.3 28.6 %collective-permute-start.1 = (bf16[128,2304]{1,0:T(8,128)(2,1)}, bf16[128,2304]{1,0:T(8,128)(2,1)S(1)}, u32[]{:S(2)}, u32[]{:S(2)}) collective-permute-start(bf16[128,2304]{1,0:T(8,128)(2,1)} %refs_0_.1), channel_id=1, source_target_pairs={{0,1},{1,2},{2,3},{3,0},{4,5},{5,6},{6,7},{7,4},{8,9},{9,10},{10,1... | collective-permute-start | bytes 1769480 | tf_op jit(solution)/shard_map/ppermute | solution.py:424
  15.3 29.4 %collective-permute-start = (bf16[128,2304]{1,0:T(8,128)(2,1)}, bf16[128,2304]{1,0:T(8,128)(2,1)S(1)}, u32[]{:S(2)}, u32[]{:S(2)}) collective-permute-start(bf16[128,2304]{1,0:T(8,128)(2,1)} %refs_0_.1), channel_id=1, source_target_pairs={{0,4},{4,0},{1,5},{5,1},{2,6},{6,2},{3,7},{7,3},{8,12},{12,8},{9,1... | collective-permute-start | bytes 1769480 | tf_op jit(solution)/shard_map/ppermute | solution.py:423
  16.0 28.7 %collective-permute-start.3 = (bf16[128,2304]{1,0:T(8,128)(2,1)}, bf16[128,2304]{1,0:T(8,128)(2,1)}, u32[]{:S(2)}, u32[]{:S(2)}) collective-permute-start(bf16[128,2304]{1,0:T(8,128)(2,1)} %refs_0_.1), channel_id=1, source_target_pairs={{0,2},{1,3},{2,0},{3,1},{4,6},{5,7},{6,4},{7,5},{8,10},{9,11},{10,... | collective-permute-start | bytes 1769480 | tf_op jit(solution)/shard_map/ppermute | solution.py:426
  45.6 36.0 %collective-permute-start.11 = (bf16[1024,2304]{1,0:T(8,128)(2,1)}, bf16[1024,2304]{1,0:T(8,128)(2,1)}, u32[]{:S(2)}, u32[]{:S(2)}) collective-permute-start(bf16[1024,2304]{1,0:T(8,128)(2,1)} %copy-done), channel_id=1, source_target_pairs={{0,8},{8,0},{1,9},{9,1},{2,10},{10,2},{3,11},{11,3},{4,12},{12,4},... | collective-permute-start | bytes 14155784 | tf_op jit(solution)/shard_map/ppermute | solution.py:439
  45.7 16.0 %collective-permute-start.7 = (bf16[128,2304]{1,0:T(8,128)(2,1)}, bf16[128,2304]{1,0:T(8,128)(2,1)S(1)}, u32[]{:S(2)}, u32[]{:S(2)}) collective-permute-start(bf16[128,2304]{1,0:T(8,128)(2,1)} %collective-permute-done.3.refs_3_), channel_id=1, source_target_pairs={{0,4},{4,0},{1,5},{5,1},{2,6},{6,2},{3,7},{7,3},{8,12},{12,8},{9,1... | collective-permute-start | bytes 1769480 | tf_op jit(solution)/shard_map/ppermute | solution.py:437
  46.5 15.4 %collective-permute-start.6 = (bf16[128,2304]{1,0:T(8,128)(2,1)S(1)}, bf16[128,2304]{1,0:T(8,128)(2,1)S(1)}, u32[]{:S(2)}, u32[]{:S(2)}) collective-permute-start(bf16[128,2304]{1,0:T(8,128)(2,1)S(1)} %collective-permute-done.refs_4_), channel_id=1, source_target_pairs={{0,3},{1,0},{2,1},{3,2},{4,7},{5,4},{6,5},{7,6},{8,11},{9,8},{10,9... | collective-permute-start | bytes 1769480 | tf_op jit(solution)/shard_map/ppermute | solution.py:436
  47.6 16.3 %collective-permute-start.5 = (bf16[128,2304]{1,0:T(8,128)(2,1)S(1)}, bf16[128,2304]{1,0:T(8,128)(2,1)S(1)}, u32[]{:S(2)}, u32[]{:S(2)}) collective-permute-start(bf16[128,2304]{1,0:T(8,128)(2,1)S(1)} %collective-permute-done.refs_4_), channel_id=1, source_target_pairs={{0,1},{1,2},{2,3},{3,0},{4,5},{5,6},{6,7},{7,4},{8,9},{9,10},{10,1... | collective-permute-start | bytes 1769480 | tf_op jit(solution)/shard_map/ppermute | solution.py:435
  48.5 12.1 %collective-permute-start.8 = (s32[1,1024]{1,0:T(1,128)S(1)}, s32[1,1024]{1,0:T(1,128)S(1)}, u32[]{:S(2)}, u32[]{:S(2)}) collective-permute-start(s32[1,1024]{1,0:T(1,128)S(1)} %bitcast.18), channel_id=1, source_target_pairs={{0,8},{8,0},{1,9},{9,1},{2,10},{10,2},{3,11},{11,3},{4,12},{12,4},... | collective-permute-start | bytes 12296 | tf_op jit(solution)/shard_map/ppermute | solution.py:441
  68.6 13.0 %collective-permute-start.10 = (bf16[8,144,1024]{2,1,0:T(8,128)(2,1)S(1)}, bf16[8,144,1024]{2,1,0:T(8,128)(2,1)S(1)}, u32[]{:S(2)}, u32[]{:S(2)}) collective-permute-start(bf16[8,144,1024]{2,1,0:T(8,128)(2,1)S(1)} %get-tuple-element.66), channel_id=1, source_target_pairs={{0,8},{8,0},{1,9},{9,1},{2,10},{10,2},{3,11},{11,3},{4,12},{12,4},... | collective-permute-start | bytes 7077896 | tf_op jit(solution)/shard_map/ppermute | solution.py:469
  69.2 3.7 %collective-permute-start.12 = (f32[32,128]{1,0:T(8,128)S(1)}, f32[32,128]{1,0:T(8,128)S(1)}, u32[]{:S(2)}, u32[]{:S(2)}) collective-permute-start(f32[32,128]{1,0:T(8,128)S(1)} %constant_dynamic-update-slice_fusion), channel_id=1, source_target_pairs={{0,4},{4,0},{1,5},{5,1},{2,6},{6,2},{3,7},{7,3},{8,12},{12,8},{9,1... | collective-permute-start | bytes 49160 | tf_op jit(solution)/shard_map/ppermute | solution.py:471
  76.7 5.0 %collective-permute-start.14 = (f32[32,128]{1,0:T(8,128)S(1)}, f32[32,128]{1,0:T(8,128)S(1)}, u32[]{:S(2)}, u32[]{:S(2)}) collective-permute-start(f32[32,128]{1,0:T(8,128)S(1)} %add.77.squares_ref), channel_id=1, source_target_pairs={{0,3},{3,0},{1,2},{2,1},{4,7},{7,4},{5,6},{6,5},{8,11},{11,8},{9,1... | collective-permute-start | bytes 49160 | tf_op jit(solution)/shard_map/ppermute | solution.py:473
  90.5 38.4 %collective-permute-start.17 = (bf16[288,1280]{1,0:T(8,128)(2,1)S(1)}, bf16[288,1280]{1,0:T(8,128)(2,1)}, u32[]{:S(2)}, u32[]{:S(2)}) collective-permute-start(bf16[288,1280]{1,0:T(8,128)(2,1)S(1)} %get-tuple-element.82), channel_id=1, source_target_pairs={{0,64},{32,96},{64,0},{96,32},{1,65},{33,97},{65,1},{97,33},{2,66}... | collective-permute-start | bytes 2211848 | tf_op jit(solution)/shard_map/ppermute | solution.py:482
  93.6 35.3 %collective-permute-start.18 = (bf16[288,1280]{1,0:T(8,128)(2,1)S(1)}, bf16[288,1280]{1,0:T(8,128)(2,1)}, u32[]{:S(2)}, u32[]{:S(2)}) collective-permute-start(bf16[288,1280]{1,0:T(8,128)(2,1)S(1)} %get-tuple-element.83), channel_id=1, source_target_pairs={{0,32},{32,64},{64,96},{96,0},{1,33},{33,65},{65,97},{97,1},{2,34}... | collective-permute-start | bytes 2211848 | tf_op jit(solution)/shard_map/ppermute | solution.py:482
  94.2 34.7 %collective-permute-start.19 = (bf16[288,1280]{1,0:T(8,128)(2,1)S(1)}, bf16[288,1280]{1,0:T(8,128)(2,1)}, u32[]{:S(2)}, u32[]{:S(2)}) collective-permute-start(bf16[288,1280]{1,0:T(8,128)(2,1)S(1)} %get-tuple-element.84), channel_id=1, source_target_pairs={{0,96},{32,0},{64,32},{96,64},{1,97},{33,1},{65,33},{97,65},{2,98}... | collective-permute-start | bytes 2211848 | tf_op jit(solution)/shard_map/ppermute | solution.py:482
  106.6 26.9 %collective-permute-start.15 = (bf16[288,1024]{1,0:T(8,128)(2,1)}, bf16[288,1024]{1,0:T(8,128)(2,1)}, u32[]{:S(2)}, u32[]{:S(2)}) collective-permute-start(bf16[288,1024]{1,0:T(8,128)(2,1)} %get-tuple-element.72), channel_id=1, source_target_pairs={{0,16},{16,0},{1,17},{17,1},{2,18},{18,2},{3,19},{19,3},{4,20},{20... | collective-permute-start | bytes 1769480 | tf_op jit(solution)/shard_map/ppermute | solution.py:484
  108.4 25.2 %collective-permute-start.16 = (bf16[288,1024]{1,0:T(8,128)(2,1)S(1)}, bf16[288,1024]{1,0:T(8,128)(2,1)}, u32[]{:S(2)}, u32[]{:S(2)}) collective-permute-start(bf16[288,1024]{1,0:T(8,128)(2,1)S(1)} %get-tuple-element.73), channel_id=1, source_target_pairs={{0,16},{16,0},{1,17},{17,1},{2,18},{18,2},{3,19},{19,3},{4,20},{20... | collective-permute-start | bytes 1769480 | tf_op jit(solution)/shard_map/ppermute | solution.py:484
  131.7 17.1 %collective-permute-start.20 = (bf16[144,1280]{1,0:T(8,128)(2,1)}, bf16[144,1280]{1,0:T(8,128)(2,1)S(1)}, u32[]{:S(2)}, u32[]{:S(2)}) collective-permute-start(bf16[144,1280]{1,0:T(8,128)(2,1)} %get-tuple-element.86), channel_id=1, source_target_pairs={{0,16},{16,0},{1,17},{17,1},{2,18},{18,2},{3,19},{19,3},{4,20},{20... | collective-permute-start | bytes 1105928 | tf_op jit(solution)/shard_map/ppermute | solution.py:493
  136.1 11.7 %collective-permute-start.21 = (bf16[144,1024]{1,0:T(8,128)(2,1)}, bf16[144,1024]{1,0:T(8,128)(2,1)S(1)}, u32[]{:S(2)}, u32[]{:S(2)}) collective-permute-start(bf16[144,1024]{1,0:T(8,128)(2,1)} %get-tuple-element.88), channel_id=1, source_target_pairs={{0,64},{32,96},{64,0},{96,32},{1,65},{33,97},{65,1},{97,33},{2,66}... | collective-permute-start | bytes 884744 | tf_op jit(solution)/shard_map/ppermute | solution.py:495
  136.2 12.1 %collective-permute-start.23 = (bf16[144,1024]{1,0:T(8,128)(2,1)}, bf16[144,1024]{1,0:T(8,128)(2,1)S(1)}, u32[]{:S(2)}, u32[]{:S(2)}) collective-permute-start(bf16[144,1024]{1,0:T(8,128)(2,1)} %get-tuple-element.89), channel_id=1, source_target_pairs={{0,96},{32,0},{64,32},{96,64},{1,97},{33,1},{65,33},{97,65},{2,98}... | collective-permute-start | bytes 884744 | tf_op jit(solution)/shard_map/ppermute | solution.py:495
  138.2 10.6 %collective-permute-start.22 = (bf16[144,1024]{1,0:T(8,128)(2,1)}, bf16[144,1024]{1,0:T(8,128)(2,1)S(1)}, u32[]{:S(2)}, u32[]{:S(2)}) collective-permute-start(bf16[144,1024]{1,0:T(8,128)(2,1)} %get-tuple-element.76.refs_0_), channel_id=1, source_target_pairs={{0,32},{32,64},{64,96},{96,0},{1,33},{33,65},{65,97},{97,1},{2,34}... | collective-permute-start | bytes 884744 | tf_op jit(solution)/shard_map/ppermute | solution.py:495
  (24 other events, 203.8 us)
Sparse Core Ops, SparseCore 0:
  9.7 44.2 all-gather.2
  56.2 34.3 all-gather.4

commit v4 on v3

--- a/solution.py
+++ b/solution.py
@@ -319,7 +319,7 @@
         out_specs=[tile(width)] * (sends + 1),
         out_shape=[jax.ShapeDtypeStruct((width, cols), jnp.float32)]
         + [jax.ShapeDtypeStruct((width, cols), jnp.bfloat16)] * sends,
-        compiler_params=params(56, "arbitrary"),
+        compiler_params=params(40, "arbitrary"),
         cost_estimate=LITTLE,
         name="add",
     )(*parts, *extra)

time: 158 us -> 159 us (level)
  waiting for transfers between devices: 30.2 us -> 34.8 us
  Pallas kernels: 68.3 us -> 66 us
  local copies, waits for them, and re-layouts: 15.7 us -> 14 us
    ppermute x2, waiting for transfers between devices: 0.11 us -> 5.01 us  [local(): got_y = [lax.ppermute(part, 'yh', shift(NY, 1)) for part in term_y[2:]]]
    pallas_call x2, Pallas kernels: 5.24 us -> 2.26 us  [add_call(): pl.pallas_call(kernel, grid=(2,), in_specs=[tile(a.shape[0]) for a in par...]
    unnamed x46 -> x40, local copies, waits for them, and re-layouts: 15.6 us -> 13.9 us
  transfers between devices with their start and end apart: 26 -> 26, of which waited for: 11 -> 10; matrix products, arithmetic and copies ran while one was open for 0% -> 0% of each run, Pallas kernels for 42% -> 41%
where the time goes in v4:
time: 159 us; the launch traced here: 158 us
  Pallas kernels  66 us (42%)
  waiting for transfers between devices  34.8 us (22%)
  starting transfers between devices  29 us (18%)
  between operations  14.3 us (9%)
  local copies, waits for them, and re-layouts  14 us (9%)
    pallas_call x2, Pallas kernels, grads_call(): pl.pallas_call(grads_kernel, grid=(steps,), in_specs=[SMEM, pl.BlockSpec(...  26.8 us
    pallas_call x2, Pallas kernels, term_call(): pl.pallas_call(functools.partial(term_kernel, clip_bound, by_x), grid=(co...  17.5 us
    unnamed x40, local copies, waits for them, and re-layouts  13.9 us
    ppermute x1, waiting for transfers between devices, local(): right = lax.ppermute(out_grad, 'z', shift(NZ, -1))  11.9 us
    pallas_call x2, Pallas kernels, gram_call(): pl.pallas_call(kernel, in_specs=[ANY] * len(pieces) + [VMEM] * (len(input...  6.57 us
    ppermute x3, starting transfers between devices, local(): lax.ppermute(term_x[dx], 'x', shift(NX, dx))  6.26 us
    pallas_call x1, Pallas kernels, hidden_gram_call(): pl.pallas_call(hidden_gram_kernel, in_specs=[SMEM, VMEM, VMEM, VMEM], out...  5.36 us
    ppermute x2, waiting for transfers between devices, local(): got_y = [lax.ppermute(part, 'yh', shift(NY, 1)) for part in term_y[2:]]  5.01 us
  transfers between devices with their start and end apart: 26, of which 10 were waited for; matrix products, arithmetic and copies ran while one was open for 0% of the time, Pallas kernels for 41%

profile of v4, /device:TPU:0, one launch (start us, length us, event | category | flops | bytes accessed | tf_op | source)
XLA Modules:
  0.0 158.2 jit_solution(14226902558812966899)
XLA Ops:
  7.9 3.4 %collective-permute-start.4 = (bf16[144,2304]{1,0:T(8,128)(2,1)}, bf16[144,2304]{1,0:T(8,128)(2,1)S(1)}, u32[]{:S(2)}, u32[]{:S(2)}) collective-permute-start(bf16[144,2304]{1,0:T(8,128)(2,1)} %bitcast.24), channel_id=1, source_target_pairs={{0,16},{16,0},{1,17},{17,1},{2,18},{18,2},{3,19},{19,3},{4,20},{20... | collective-permute-start | bytes 1990664 | tf_op jit(solution)/shard_map/ppermute | solution.py:420
  11.3 4.0 %collective-permute-start.2 = (bf16[128,2304]{1,0:T(8,128)(2,1)}, bf16[128,2304]{1,0:T(8,128)(2,1)S(1)}, u32[]{:S(2)}, u32[]{:S(2)}) collective-permute-start(bf16[128,2304]{1,0:T(8,128)(2,1)} %refs_0_.1), channel_id=1, source_target_pairs={{0,3},{1,0},{2,1},{3,2},{4,7},{5,4},{6,5},{7,6},{8,11},{9,8},{10,9... | collective-permute-start | bytes 1769480 | tf_op jit(solution)/shard_map/ppermute | solution.py:425
  17.9 2.3 %copy-done.3 = bf16[1024,2304]{1,0:T(8,128)(2,1)S(1)} copy-done((bf16[1024,2304]{1,0:T(8,128)(2,1)S(1)}, bf16[1024,2304]{1,0:T(8,128)(2,1)}, u32[]{:S(2)}) %copy-start.3) | copy-done | bytes 4718616
  20.2 2.7 %copy-done.4 = bf16[1024,2304]{1,0:T(8,128)(2,1)S(1)} copy-done((bf16[1024,2304]{1,0:T(8,128)(2,1)S(1)}, bf16[1024,2304]{1,0:T(8,128)(2,1)}, u32[]{:S(2)}) %copy-start.4) | copy-done | bytes 4718616
  22.9 3.6 %hidden.1.hidden_ref.own_ref = bf16[1024,2304]{1,0:T(8,128)(2,1)S(1)} custom-call(bf16[1024,2304]{1,0:T(8,128)(2,1)S(1)} %copy-done.3, bf16[1024,2304]{1,0:T(8,128)(2,1)S(1)} %copy-done.4), custom_call_target="tpu_custom_call" | custom-call | flops 1 | bytes 1 | tf_op jit(solution)/shard_map/hidden/pallas_call | solution.py:57
  26.6 2.2 %copy-done = bf16[1024,2304]{1,0:T(8,128)(2,1)} copy-done((bf16[1024,2304]{1,0:T(8,128)(2,1)}, bf16[1024,2304]{1,0:T(8,128)(2,1)S(1)}, u32[]{:S(2)}) %copy-start) | copy-done | bytes 4718616
  28.8 11.9 %collective-permute-done.2.refs_2_ = bf16[128,2304]{1,0:T(8,128)(2,1)S(1)} collective-permute-done((bf16[128,2304]{1,0:T(8,128)(2,1)}, bf16[128,2304]{1,0:T(8,128)(2,1)S(1)}, u32[]{:S(2)}, u32[]{:S(2)}) %collective-permute-start.2) | collective-permute-done | bytes 589856 | tf_op jit(solution)/shard_map/ppermute | solution.py:425
  41.4 2.5 %collective-permute-done.1.refs_1_ = bf16[128,2304]{1,0:T(8,128)(2,1)S(1)} collective-permute-done((bf16[128,2304]{1,0:T(8,128)(2,1)}, bf16[128,2304]{1,0:T(8,128)(2,1)S(1)}, u32[]{:S(2)}, u32[]{:S(2)}) %collective-permute-start.1) | collective-permute-done | bytes 589856 | tf_op jit(solution)/shard_map/ppermute | solution.py:424
  48.8 2.3 %copy-done.1 = bf16[1024,2304]{1,0:T(8,128)(2,1)S(1)} copy-done((bf16[1024,2304]{1,0:T(8,128)(2,1)S(1)}, bf16[1024,2304]{1,0:T(8,128)(2,1)}, u32[]{:S(2)}) %copy-start.1) | copy-done | bytes 4718616
  51.2 5.4 %hidden_gram.1 = (f32[640,640]{1,0:T(8,128)S(1)}, f32[384,1024]{1,0:T(8,128)S(1)}, s32[1,1024]{1,0:T(1,128)S(1)}) custom-call(s32[11]{0:T(128)S(1)} %stack.47.place_ref.after_ref, bf16[1024,2304]{1,0:T(8,128)(2,1)S(1)} %copy-done.1, s32[1024,1]{1,0:T(8,128)S(1)} %copy.12.user_ref, s32[1,1024]{1,0:T(1,128)S(1)} %bitcast.19), custom_call_target="tpu_custom_call" | custom-call | flops 1 | bytes 1 | tf_op jit(solution)/shard_map/hidden_gram/pallas_call | solution.py:100
  56.6 4.0 %early_gram.1 = (bf16[1024,2304]{1,0:T(8,128)(2,1)S(1)}, f32[16,128]{1,0:T(8,128)S(1)}) custom-call(bf16[128,2304]{1,0:T(8,128)(2,1)S(1)} %copy-done.6, bf16[128,2304]{1,0:T(8,128)(2,1)S(1)} %copy-done.10, bf16[128,2304]{1,0:T(8,128)(2,1)S(1)} %copy-done.8, bf16[128,2304]{1,0:T(8,128)(2,1)} %collective-permute-done.3.refs_3_, ...), custom_call_target="tpu_custom_call" | custom-call | flops 1 | bytes 1 | tf_op jit(solution)/shard_map/early_gram/pallas_call | solution.py:155
  61.8 2.0 %collective-permute-done.5.refs_0_ = bf16[128,2304]{1,0:T(8,128)(2,1)S(1)} collective-permute-done((bf16[128,2304]{1,0:T(8,128)(2,1)S(1)}, bf16[128,2304]{1,0:T(8,128)(2,1)S(1)}, u32[]{:S(2)}, u32[]{:S(2)}) %collective-permute-start.5) | collective-permute-done | bytes 589856 | tf_op jit(solution)/shard_map/ppermute | solution.py:435
  63.9 2.5 %late_gram.1 = (bf16[1024,2304]{1,0:T(8,128)(2,1)S(1)}, f32[16,128]{1,0:T(8,128)S(1)}) custom-call(bf16[128,2304]{1,0:T(8,128)(2,1)S(1)} %collective-permute-done.5.refs_0_, bf16[128,2304]{1,0:T(8,128)(2,1)S(1)} %collective-permute-done.6.refs_1_, bf16[128,2304]{1,0:T(8,128)(2,1)S(1)} %collective-permute-done.7.refs_2_, ...), custom_call_target="tpu_custom_call", output_to_operand_aliasing={{0}: (6, {})} | custom-call | flops 1 | bytes 1 | tf_op jit(solution)/shard_map/late_gram/pallas_call | solution.py:155
  66.5 2.1 %transpose.17 = (bf16[8,144,1024]{2,1,0:T(8,128)(2,1)S(1)}, bf16[8,144,1024]{2,1,0:T(8,128)(2,1)S(1)}) custom-call(s32[11]{0:T(128)S(1)} %stack.47.place_ref.after_ref, bf16[1024,2304]{1,0:T(8,128)(2,1)S(1)} %get-tuple-element.61.grad_ref.blocks_ref), custom_call_target="tpu_custom_call" | custom-call | flops 1 | bytes 1 | tf_op jit(solution)/shard_map/transpose/pallas_call | solution.py:190
  70.6 2.4 %collective-permute-done.12 = f32[32,128]{1,0:T(8,128)S(1)} collective-permute-done((f32[32,128]{1,0:T(8,128)S(1)}, f32[32,128]{1,0:T(8,128)S(1)}, u32[]{:S(2)}, u32[]{:S(2)}) %collective-permute-start.12) | collective-permute-done | bytes 16416 | tf_op jit(solution)/shard_map/ppermute | solution.py:471
  73.0 3.7 %collective-permute-done.13 = f32[32,128]{1,0:T(8,128)S(1)} collective-permute-done((f32[32,128]{1,0:T(8,128)S(1)}, f32[32,128]{1,0:T(8,128)S(1)}, u32[]{:S(2)}, u32[]{:S(2)}) %collective-permute-start.13) | collective-permute-done | bytes 16416 | tf_op jit(solution)/shard_map/ppermute | solution.py:472
  77.0 4.7 %collective-permute-done.14.more_ref = f32[32,128]{1,0:T(8,128)S(1)} collective-permute-done((f32[32,128]{1,0:T(8,128)S(1)}, f32[32,128]{1,0:T(8,128)S(1)}, u32[]{:S(2)}, u32[]{:S(2)}) %collective-permute-start.14) | collective-permute-done | bytes 16416 | tf_op jit(solution)/shard_map/ppermute | solution.py:473
  81.7 9.5 %term_x.1 = (bf16[288,1280]{1,0:T(8,128)(2,1)S(1)}, bf16[288,1280]{1,0:T(8,128)(2,1)}, bf16[288,1280]{1,0:T(8,128)(2,1)}, bf16[288,1280]{1,0:T(8,128)(2,1)}, f32[8,128]{1,0:T(8,128)S(1)}) custom-call(s32[11]{0:T(128)S(1)} %stack.47.place_ref.after_ref, bf16[8,144,1024]{2,1,0:T(8,128)(2,1)S(1)} %get-tuple-element.63.mine_ref, ...), custom_call_target="tpu_custom_call" | custom-call | flops 1 | bytes 1 | tf_op jit(solution)/shard_map/term_x/pallas_call | solution.py:280
  91.2 3.0 %collective-permute-start.17 = (bf16[288,1280]{1,0:T(8,128)(2,1)}, bf16[288,1280]{1,0:T(8,128)(2,1)S(1)}, u32[]{:S(2)}, u32[]{:S(2)}) collective-permute-start(bf16[288,1280]{1,0:T(8,128)(2,1)} %get-tuple-element.82), channel_id=1, source_target_pairs={{0,64},{32,96},{64,0},{96,32},{1,65},{33,97},{65,1},{97,33},{2,66}... | collective-permute-start | bytes 2211848 | tf_op jit(solution)/shard_map/ppermute | solution.py:482
  94.8 2.6 %collective-permute-start.19 = (bf16[288,1280]{1,0:T(8,128)(2,1)}, bf16[288,1280]{1,0:T(8,128)(2,1)S(1)}, u32[]{:S(2)}, u32[]{:S(2)}) collective-permute-start(bf16[288,1280]{1,0:T(8,128)(2,1)} %get-tuple-element.84), channel_id=1, source_target_pairs={{0,96},{32,0},{64,32},{96,64},{1,97},{33,1},{65,33},{97,65},{2,98}... | collective-permute-start | bytes 2211848 | tf_op jit(solution)/shard_map/ppermute | solution.py:482
  97.4 8.0 %term_y.1 = (bf16[288,1024]{1,0:T(8,128)(2,1)S(1)}, bf16[288,1024]{1,0:T(8,128)(2,1)S(1)}, bf16[288,1024]{1,0:T(8,128)(2,1)}, bf16[288,1024]{1,0:T(8,128)(2,1)}, f32[8,128]{1,0:T(8,128)S(1)}) custom-call(s32[11]{0:T(128)S(1)} %stack.47.place_ref.after_ref, bf16[8,144,1024]{2,1,0:T(8,128)(2,1)S(1)} %get-tuple-element.63.mine_ref, ...), custom_call_target="tpu_custom_call" | custom-call | flops 1 | bytes 1 | tf_op jit(solution)/shard_map/term_y/pallas_call | solution.py:280
  110.6 18.3 %grads.2 = (bf16[1024,2304]{1,0:T(8,128)(2,1)}, bf16[1024,2304]{1,0:T(8,128)(2,1)}, f32[8,128]{1,0:T(8,128)S(1)}) custom-call(s32[11]{0:T(128)S(1)} %stack.47.place_ref.after_ref, bf16[1024,2304]{1,0:T(8,128)(2,1)} %copy-done.2, bf16[1152,2304]{1,0:T(8,128)(2,1)} %all-gather.3.cloned.1.call-done.same_ref, ...), custom_call_target="tpu_custom_call" | custom-call | flops 1 | bytes 1 | tf_op jit(solution)/shard_map/grads/pallas_call | solution.py:358
  131.6 5.0 %collective-permute-done.16.second_high = bf16[288,1024]{1,0:T(8,128)(2,1)} collective-permute-done((bf16[288,1024]{1,0:T(8,128)(2,1)}, bf16[288,1024]{1,0:T(8,128)(2,1)}, u32[]{:S(2)}, u32[]{:S(2)}) %collective-permute-start.16) | collective-permute-done | bytes 589856 | tf_op jit(solution)/shard_map/ppermute | solution.py:484
  140.3 8.5 %grads.3 = (bf16[1024,2304]{1,0:T(8,128)(2,1)}, bf16[1024,2304]{1,0:T(8,128)(2,1)}, f32[8,128]{1,0:T(8,128)S(1)}) custom-call(s32[11]{0:T(128)S(1)} %stack.47.place_ref.after_ref, bf16[1024,2304]{1,0:T(8,128)(2,1)} %copy-done.2, bf16[1152,2304]{1,0:T(8,128)(2,1)} %all-gather.3.cloned.1.call-done.same_ref, ...), custom_call_target="tpu_custom_call", output_to_operand_aliasing={{0}: (7, {}), {1}: (8, {})} | custom-call | flops 1 | bytes 1 | tf_op jit(solution)/shard_map/grads/pallas_call | solution.py:358
  (87 shorter events, 27.1 us)
Async XLA Ops:
  7.2 103.4 %all-gather.3.cloned.1.call-start = ((), (), s32[]{:S(2)}) async-start(), calls=%async_computation | async-start | bytes 5971968 | tf_op jit(solution)/shard_map/all_gather | solution.py:433
  7.9 102.7 %all-gather.5.cloned.1.call-start = ((), (), s32[]{:S(2)}) async-start(), calls=%async_computation.1 | async-start | bytes 5971968 | tf_op jit(solution)/shard_map/all_gather | solution.py:433
  7.9 36.8 %collective-permute-start.4 = (bf16[144,2304]{1,0:T(8,128)(2,1)}, bf16[144,2304]{1,0:T(8,128)(2,1)S(1)}, u32[]{:S(2)}, u32[]{:S(2)}) collective-permute-start(bf16[144,2304]{1,0:T(8,128)(2,1)} %bitcast.24), channel_id=1, source_target_pairs={{0,16},{16,0},{1,17},{17,1},{2,18},{18,2},{3,19},{19,3},{4,20},{20... | collective-permute-start | bytes 1990664 | tf_op jit(solution)/shard_map/ppermute | solution.py:420
  11.3 29.3 %collective-permute-start.2 = (bf16[128,2304]{1,0:T(8,128)(2,1)}, bf16[128,2304]{1,0:T(8,128)(2,1)S(1)}, u32[]{:S(2)}, u32[]{:S(2)}) collective-permute-start(bf16[128,2304]{1,0:T(8,128)(2,1)} %refs_0_.1), channel_id=1, source_target_pairs={{0,3},{1,0},{2,1},{3,2},{4,7},{5,4},{6,5},{7,6},{8,11},{9,8},{10,9... | collective-permute-start | bytes 1769480 | tf_op jit(solution)/shard_map/ppermute | solution.py:425
  15.3 28.6 %collective-permute-start.1 = (bf16[128,2304]{1,0:T(8,128)(2,1)}, bf16[128,2304]{1,0:T(8,128)(2,1)S(1)}, u32[]{:S(2)}, u32[]{:S(2)}) collective-permute-start(bf16[128,2304]{1,0:T(8,128)(2,1)} %refs_0_.1), channel_id=1, source_target_pairs={{0,1},{1,2},{2,3},{3,0},{4,5},{5,6},{6,7},{7,4},{8,9},{9,10},{10,1... | collective-permute-start | bytes 1769480 | tf_op jit(solution)/shard_map/ppermute | solution.py:424
  15.3 29.4 %collective-permute-start = (bf16[128,2304]{1,0:T(8,128)(2,1)}, bf16[128,2304]{1,0:T(8,128)(2,1)S(1)}, u32[]{:S(2)}, u32[]{:S(2)}) collective-permute-start(bf16[128,2304]{1,0:T(8,128)(2,1)} %refs_0_.1), channel_id=1, source_target_pairs={{0,4},{4,0},{1,5},{5,1},{2,6},{6,2},{3,7},{7,3},{8,12},{12,8},{9,1... | collective-permute-start | bytes 1769480 | tf_op jit(solution)/shard_map/ppermute | solution.py:423
  16.0 28.7 %collective-permute-start.3 = (bf16[128,2304]{1,0:T(8,128)(2,1)}, bf16[128,2304]{1,0:T(8,128)(2,1)}, u32[]{:S(2)}, u32[]{:S(2)}) collective-permute-start(bf16[128,2304]{1,0:T(8,128)(2,1)} %refs_0_.1), channel_id=1, source_target_pairs={{0,2},{1,3},{2,0},{3,1},{4,6},{5,7},{6,4},{7,5},{8,10},{9,11},{10,... | collective-permute-start | bytes 1769480 | tf_op jit(solution)/shard_map/ppermute | solution.py:426
  45.6 36.1 %collective-permute-start.11 = (bf16[1024,2304]{1,0:T(8,128)(2,1)}, bf16[1024,2304]{1,0:T(8,128)(2,1)}, u32[]{:S(2)}, u32[]{:S(2)}) collective-permute-start(bf16[1024,2304]{1,0:T(8,128)(2,1)} %copy-done), channel_id=1, source_target_pairs={{0,8},{8,0},{1,9},{9,1},{2,10},{10,2},{3,11},{11,3},{4,12},{12,4},... | collective-permute-start | bytes 14155784 | tf_op jit(solution)/shard_map/ppermute | solution.py:439
  45.7 16.0 %collective-permute-start.7 = (bf16[128,2304]{1,0:T(8,128)(2,1)}, bf16[128,2304]{1,0:T(8,128)(2,1)S(1)}, u32[]{:S(2)}, u32[]{:S(2)}) collective-permute-start(bf16[128,2304]{1,0:T(8,128)(2,1)} %collective-permute-done.3.refs_3_), channel_id=1, source_target_pairs={{0,4},{4,0},{1,5},{5,1},{2,6},{6,2},{3,7},{7,3},{8,12},{12,8},{9,1... | collective-permute-start | bytes 1769480 | tf_op jit(solution)/shard_map/ppermute | solution.py:437
  46.5 15.4 %collective-permute-start.6 = (bf16[128,2304]{1,0:T(8,128)(2,1)S(1)}, bf16[128,2304]{1,0:T(8,128)(2,1)S(1)}, u32[]{:S(2)}, u32[]{:S(2)}) collective-permute-start(bf16[128,2304]{1,0:T(8,128)(2,1)S(1)} %collective-permute-done.refs_4_), channel_id=1, source_target_pairs={{0,3},{1,0},{2,1},{3,2},{4,7},{5,4},{6,5},{7,6},{8,11},{9,8},{10,9... | collective-permute-start | bytes 1769480 | tf_op jit(solution)/shard_map/ppermute | solution.py:436
  47.6 16.3 %collective-permute-start.5 = (bf16[128,2304]{1,0:T(8,128)(2,1)S(1)}, bf16[128,2304]{1,0:T(8,128)(2,1)S(1)}, u32[]{:S(2)}, u32[]{:S(2)}) collective-permute-start(bf16[128,2304]{1,0:T(8,128)(2,1)S(1)} %collective-permute-done.refs_4_), channel_id=1, source_target_pairs={{0,1},{1,2},{2,3},{3,0},{4,5},{5,6},{6,7},{7,4},{8,9},{9,10},{10,1... | collective-permute-start | bytes 1769480 | tf_op jit(solution)/shard_map/ppermute | solution.py:435
  48.5 12.1 %collective-permute-start.8 = (s32[1,1024]{1,0:T(1,128)S(1)}, s32[1,1024]{1,0:T(1,128)S(1)}, u32[]{:S(2)}, u32[]{:S(2)}) collective-permute-start(s32[1,1024]{1,0:T(1,128)S(1)} %bitcast.18), channel_id=1, source_target_pairs={{0,8},{8,0},{1,9},{9,1},{2,10},{10,2},{3,11},{11,3},{4,12},{12,4},... | collective-permute-start | bytes 12296 | tf_op jit(solution)/shard_map/ppermute | solution.py:441
  68.6 13.0 %collective-permute-start.10 = (bf16[8,144,1024]{2,1,0:T(8,128)(2,1)S(1)}, bf16[8,144,1024]{2,1,0:T(8,128)(2,1)S(1)}, u32[]{:S(2)}, u32[]{:S(2)}) collective-permute-start(bf16[8,144,1024]{2,1,0:T(8,128)(2,1)S(1)} %get-tuple-element.66), channel_id=1, source_target_pairs={{0,8},{8,0},{1,9},{9,1},{2,10},{10,2},{3,11},{11,3},{4,12},{12,4},... | collective-permute-start | bytes 7077896 | tf_op jit(solution)/shard_map/ppermute | solution.py:469
  69.2 3.7 %collective-permute-start.12 = (f32[32,128]{1,0:T(8,128)S(1)}, f32[32,128]{1,0:T(8,128)S(1)}, u32[]{:S(2)}, u32[]{:S(2)}) collective-permute-start(f32[32,128]{1,0:T(8,128)S(1)} %constant_dynamic-update-slice_fusion), channel_id=1, source_target_pairs={{0,4},{4,0},{1,5},{5,1},{2,6},{6,2},{3,7},{7,3},{8,12},{12,8},{9,1... | collective-permute-start | bytes 49160 | tf_op jit(solution)/shard_map/ppermute | solution.py:471
  76.7 5.0 %collective-permute-start.14 = (f32[32,128]{1,0:T(8,128)S(1)}, f32[32,128]{1,0:T(8,128)S(1)}, u32[]{:S(2)}, u32[]{:S(2)}) collective-permute-start(f32[32,128]{1,0:T(8,128)S(1)} %add.77.squares_ref), channel_id=1, source_target_pairs={{0,3},{3,0},{1,2},{2,1},{4,7},{7,4},{5,6},{6,5},{8,11},{11,8},{9,1... | collective-permute-start | bytes 49160 | tf_op jit(solution)/shard_map/ppermute | solution.py:473
  91.2 37.8 %collective-permute-start.17 = (bf16[288,1280]{1,0:T(8,128)(2,1)}, bf16[288,1280]{1,0:T(8,128)(2,1)S(1)}, u32[]{:S(2)}, u32[]{:S(2)}) collective-permute-start(bf16[288,1280]{1,0:T(8,128)(2,1)} %get-tuple-element.82), channel_id=1, source_target_pairs={{0,64},{32,96},{64,0},{96,32},{1,65},{33,97},{65,1},{97,33},{2,66}... | collective-permute-start | bytes 2211848 | tf_op jit(solution)/shard_map/ppermute | solution.py:482
  94.2 34.7 %collective-permute-start.18 = (bf16[288,1280]{1,0:T(8,128)(2,1)}, bf16[288,1280]{1,0:T(8,128)(2,1)S(1)}, u32[]{:S(2)}, u32[]{:S(2)}) collective-permute-start(bf16[288,1280]{1,0:T(8,128)(2,1)} %get-tuple-element.83), channel_id=1, source_target_pairs={{0,32},{32,64},{64,96},{96,0},{1,33},{33,65},{65,97},{97,1},{2,34}... | collective-permute-start | bytes 2211848 | tf_op jit(solution)/shard_map/ppermute | solution.py:482
  94.8 34.2 %collective-permute-start.19 = (bf16[288,1280]{1,0:T(8,128)(2,1)}, bf16[288,1280]{1,0:T(8,128)(2,1)S(1)}, u32[]{:S(2)}, u32[]{:S(2)}) collective-permute-start(bf16[288,1280]{1,0:T(8,128)(2,1)} %get-tuple-element.84), channel_id=1, source_target_pairs={{0,96},{32,0},{64,32},{96,64},{1,97},{33,1},{65,33},{97,65},{2,98}... | collective-permute-start | bytes 2211848 | tf_op jit(solution)/shard_map/ppermute | solution.py:482
  107.1 24.6 %collective-permute-start.15 = (bf16[288,1024]{1,0:T(8,128)(2,1)}, bf16[288,1024]{1,0:T(8,128)(2,1)}, u32[]{:S(2)}, u32[]{:S(2)}) collective-permute-start(bf16[288,1024]{1,0:T(8,128)(2,1)} %get-tuple-element.72), channel_id=1, source_target_pairs={{0,16},{16,0},{1,17},{17,1},{2,18},{18,2},{3,19},{19,3},{4,20},{20... | collective-permute-start | bytes 1769480 | tf_op jit(solution)/shard_map/ppermute | solution.py:484
  108.9 27.7 %collective-permute-start.16 = (bf16[288,1024]{1,0:T(8,128)(2,1)}, bf16[288,1024]{1,0:T(8,128)(2,1)}, u32[]{:S(2)}, u32[]{:S(2)}) collective-permute-start(bf16[288,1024]{1,0:T(8,128)(2,1)} %get-tuple-element.73), channel_id=1, source_target_pairs={{0,16},{16,0},{1,17},{17,1},{2,18},{18,2},{3,19},{19,3},{4,20},{20... | collective-permute-start | bytes 1769480 | tf_op jit(solution)/shard_map/ppermute | solution.py:484
  129.7 19.9 %collective-permute-start.20 = (bf16[144,1280]{1,0:T(8,128)(2,1)S(1)}, bf16[144,1280]{1,0:T(8,128)(2,1)S(1)}, u32[]{:S(2)}, u32[]{:S(2)}) collective-permute-start(bf16[144,1280]{1,0:T(8,128)(2,1)S(1)} %get-tuple-element.86), channel_id=1, source_target_pairs={{0,16},{16,0},{1,17},{17,1},{2,18},{18,2},{3,19},{19,3},{4,20},{20... | collective-permute-start | bytes 1105928 | tf_op jit(solution)/shard_map/ppermute | solution.py:493
  138.2 10.7 %collective-permute-start.21 = (bf16[144,1024]{1,0:T(8,128)(2,1)S(1)}, bf16[144,1024]{1,0:T(8,128)(2,1)S(1)}, u32[]{:S(2)}, u32[]{:S(2)}) collective-permute-start(bf16[144,1024]{1,0:T(8,128)(2,1)S(1)} %get-tuple-element.88), channel_id=1, source_target_pairs={{0,64},{32,96},{64,0},{96,32},{1,65},{33,97},{65,1},{97,33},{2,66}... | collective-permute-start | bytes 884744 | tf_op jit(solution)/shard_map/ppermute | solution.py:495
  138.3 10.6 %collective-permute-start.23 = (bf16[144,1024]{1,0:T(8,128)(2,1)S(1)}, bf16[144,1024]{1,0:T(8,128)(2,1)S(1)}, u32[]{:S(2)}, u32[]{:S(2)}) collective-permute-start(bf16[144,1024]{1,0:T(8,128)(2,1)S(1)} %get-tuple-element.89), channel_id=1, source_target_pairs={{0,96},{32,0},{64,32},{96,64},{1,97},{33,1},{65,33},{97,65},{2,98}... | collective-permute-start | bytes 884744 | tf_op jit(solution)/shard_map/ppermute | solution.py:495
  139.3 10.3 %collective-permute-start.22 = (bf16[144,1024]{1,0:T(8,128)(2,1)S(1)}, bf16[144,1024]{1,0:T(8,128)(2,1)S(1)}, u32[]{:S(2)}, u32[]{:S(2)}) collective-permute-start(bf16[144,1024]{1,0:T(8,128)(2,1)S(1)} %get-tuple-element.76.refs_0_), channel_id=1, source_target_pairs={{0,32},{32,64},{64,96},{96,0},{1,33},{33,65},{65,97},{97,1},{2,34}... | collective-permute-start | bytes 884744 | tf_op jit(solution)/shard_map/ppermute | solution.py:495
  (21 other events, 221.1 us)
Sparse Core Ops, SparseCore 0:
  9.7 44.2 all-gather.2
  56.2 34.4 all-gather.4
